TPU v7x, 32 devices: a whole 2x2x4 slice. The times are simulated.
32 devices in a mesh: quad: 4 (over z), row: 8 (over y, x, core).
Axes of the slice: x: 2, y: 2, z: 4, core: 2. Of those that a mesh axis runs over, the one named last changes fastest.
Arguments:
- hamiltonian: bfloat16 [512, 64, 1536], P('row'), may hold values from -0.15625 to 0.15625
- columns: int32 [512, 24], P('row'), may hold values from 0 to 511, as said below
- counts: int32 [512], P('row'), may hold values from 2 to 24, as said below
- precond: bfloat16 [8, 512, 64, 128], P('quad', 'row'), may hold values from -0.5 to 0.5
- rhs: bfloat16 [32768, 128], P('row'), may hold values from -6 to 6
Outputs:
- moments_out: float32 [8, 32768, 128], P('quad', 'row')
- blocks_out: float32 [8, 128, 128], P('quad')
Inputs may be any that keep to these rules, and one draw needn't show every extreme that they name: `columns`: slot 0 of row block b holds b itself; slot 1 holds b - 64 for even b and b + 64 for odd b, reflected at the ends (an index -m becomes m, an index 511 + m becomes 512 - 1 - m); every column block lies within 64 blocks of its row block. `counts`: every run of 64 row blocks starting at a multiple of 64 holds a row block with all 24 slots live.
All inputs are finite; a program needn't handle non-finite values.
Results may differ from a plain program's by a relative error of at most 0.02.
Values may be sent and summed in bfloat16 or wider, within the bound.
A program may use at most 128 MiB of HBM per device.

v0:
```python
import math

import jax
import jax.numpy as jnp
from jax import lax
from jax.sharding import PartitionSpec as P

ITERS = 2
MOMENTS = 8


def extended_2(x, sides, width):
    for axis, dim in sides:
        peers, length = (lax.axis_size(axis), x.shape[dim])
        up = [(i, (i + 1) % peers) for i in range(peers - 1)]
        down = [(j, i) for i, j in up]
        last = lax.slice_in_dim(x, length - width, length, axis=dim)
        first = lax.slice_in_dim(x, 0, width, axis=dim)
        before = lax.ppermute(last, axis, up)
        after = lax.ppermute(first, axis, down)
        x = jnp.concatenate([before, x, after], axis=dim)
    return x


def rotate(values):
    half_cols = values.shape[-1] // 2
    return jnp.concatenate([-values[..., half_cols:], values[..., :half_cols]], axis=-1)


def precondition(blocks_pre, resid):
    stacked = jnp.concatenate([resid, rotate(resid)], axis=1)
    return jnp.einsum("bij,bjc->bic", blocks_pre, stacked, preferred_element_type=jnp.float32)


def shards(hamiltonian, columns, counts, precond, rhs):
    row_blocks = hamiltonian.shape[0]
    block_size = hamiltonian.shape[1]
    slots = columns.shape[1]
    width = rhs.shape[1]
    per_quad = precond.shape[0]
    quad_count = lax.axis_size("quad")
    row_count = lax.axis_size("row")
    quads_total = per_quad * quad_count
    per_device = MOMENTS // quad_count
    local_rows = row_blocks * block_size
    row_index = lax.axis_index("row")
    quad_index = lax.axis_index("quad")
    first_block = (row_index - 1) * row_blocks
    live = jnp.arange(slots)[None, :] < counts[:, None]
    local_index = jnp.where(live, columns - first_block, 3 * row_blocks)
    rhs_blocks = rhs.reshape(row_blocks, block_size, width)
    rhs_float = rhs_blocks.astype(jnp.float32)
    thetas = []
    solutions = []
    for which in range(per_quad):
        theta = (
            2.0 * jnp.pi * ((quad_index * per_quad + which).astype(jnp.float32) + 0.5) / quads_total
        )
        thetas.append(theta)
        zreal = jnp.cos(theta)
        zimag = jnp.sin(theta)
        iterate = precondition(precond[which], rhs_blocks).astype(jnp.bfloat16)
        for sweep in range(ITERS):
            flat = iterate.reshape(local_rows, width)
            extended = extended_2(flat, (("row", 0),), local_rows)
            stacked = jnp.concatenate(
                [
                    extended.reshape(3 * row_blocks, block_size, width),
                    jnp.zeros((1, block_size, width), jnp.bfloat16),
                ],
                axis=0,
            )
            gathered = stacked[local_index].reshape(row_blocks, slots * block_size, width)
            product = jnp.einsum(
                "bij,bjc->bic", hamiltonian, gathered, preferred_element_type=jnp.float32
            )
            current = iterate.astype(jnp.float32)
            shifted = zreal * current + zimag * rotate(current)
            resid = (rhs_float - (shifted - product)).astype(jnp.bfloat16)
            iterate = (current + precondition(precond[which], resid)).astype(jnp.bfloat16)
        solutions.append(iterate.reshape(local_rows, width))
    orders = jnp.arange(lax.axis_size("quad") * per_device).astype(jnp.float32) + 1.0
    total = jnp.zeros((lax.axis_size("quad") * per_device, local_rows, width), jnp.float32)
    for which in range(per_quad):
        phase = orders * thetas[which]
        coef_a = jnp.cos(phase) / quads_total
        coef_b = jnp.sin(phase) / quads_total
        current = solutions[which].astype(jnp.float32)
        total = (
            total
            + coef_a[:, None, None] * current[None]
            + coef_b[:, None, None] * rotate(current)[None]
        )
    held = lax.optimization_barrier(total.astype(jnp.bfloat16))
    moments_out = lax.psum_scatter(
        held.astype(jnp.float32).astype(jnp.bfloat16), "quad", scatter_dimension=0, tiled=True
    ).astype(jnp.float32)
    scale = 1.0 / math.sqrt(local_rows * row_count)
    flat_rhs = rhs.astype(jnp.float32)
    local_blocks = (
        jnp.einsum("rc,krd->kcd", flat_rhs, moments_out, precision=lax.Precision.HIGHEST) * scale
    )
    blocks_out = lax.psum(local_blocks.astype(jnp.bfloat16), "row").astype(jnp.float32)
    return (moments_out, blocks_out)


def solution(mesh):
    return jax.shard_map(
        shards,
        mesh=mesh,
        in_specs=(
            P("row", None, None),
            P("row", None),
            P("row"),
            P("quad", "row", None, None),
            P("row", None),
        ),
        out_specs=(P("quad", "row", None), P("quad", None, None)),
        check_vma=False,
    )
```

profile of v0, /device:TPU:0, one launch (start us, length us, event | category | flops | bytes accessed | tf_op | source)
XLA Modules:
  0.0 522.0 jit_solution(13062682737847708148)
XLA Ops:
  7.2 2.1 slice_negate_fusion.10
  9.4 0.4 copy-done.9
  9.8 0.7 bitcast_convert_fusion.1
  10.5 3.5 collective-permute-start.4
  14.1 1.3 collective-permute-start.5
  15.4 2.4 bitcast_convert_fusion.3
  17.8 5.1 collective-permute-start
  22.9 1.3 collective-permute-start.1
  24.5 0.1 copy.9
  24.6 0.1 reshape.100
  24.7 0.6 sine_multiply_fusion
  25.3 0.6 sine_multiply_fusion.1
  25.9 2.8 slice_negate_fusion.2
  28.7 2.8 slice_negate_fusion.5
  31.6 9.0 %pad_maximum_fusion.2 = bf16[12288,128]{1,0:T(8,128)(2,1)S(1)} fusion(bf16[4096,128]{1,0:T(8,128)(2,1)} %collective-permute-done.5, bf16[4096,128]{1,0:T(8,128)(2,1)S(1)} %bitcast.106, bf16[4096,128]{1,0:T(8,128)(2,1)} %collective-permute-done.4), kind=kLoop, calls=%fused_computation.11 | loop fusion | flops 9437184 | bytes 6291456 | tf_op jit(solution)/shard_map/concatenate | solution.py:21
  40.5 0.7 concatenate.89
  41.2 31.9 %gather_fusion.2 = bf16[1536,64,128]{2,1,0:T(8,128)(2,1)} fusion(bf16[193,64,128]{2,1,0:T(8,128)(2,1)S(1)} %concatenate.89, s32[2048]{0:T(1024)S(1)} %pad_clamp_fusion), kind=kCustom, calls=%fused_computation.2 | custom fusion | bytes 50337792 | tf_op jit(solution)/shard_map/gather | solution.py:73
  73.2 16.3 %fusion.2 = bf16[64,64,128]{2,1,0:T(8,128)(2,1)S(1)} fusion(bf16[64,64,128]{2,1,0:T(8,128)(2,1)} %bitcast.98, f32[64,64,64]{2,1,0:T(8,128)} %get-tuple-element.13, f32[64,64,64]{2,1,0:T(8,128)} %get-tuple-element.12, bf16[64,64,1536]{2,1,0:T(8,128)(2,1)} %param.5, bf16[64,1536,128]{2,1,0:T(8,128)(2,1)} %bitcast.95, bf16[64,128,64]{1,2,0:T(8,128)(2,1)} %copy-done.5, ...), kind=kOutput, calls=%fused_computation.15 | convolution fusion | flops 1615331328 | bytes 42991624 | tf_op jit(solution)/shard_map/bij,bjc->bic/dot_general | solution.py:74
  89.5 0.4 slice_negate_fusion.7
  89.9 0.8 copy-done.6
  90.7 0.7 copy-done.10
  91.4 2.5 fusion.71
  93.9 14.6 %collective-permute-start.6 = (bf16[4096,128]{1,0:T(8,128)(2,1)}, bf16[4096,128]{1,0:T(8,128)(2,1)}, u32[]{:S(2)}, u32[]{:S(2)}) collective-permute-start(bf16[4096,128]{1,0:T(8,128)(2,1)} %bitcast.24), channel_id=1, source_target_pairs={{0,1},{1,2},{2,3},{3,4},{4,5},{5,6},{6,7},{8,9},{9,10},{10,11},{11... | collective-permute-start | bytes 3145736 | tf_op jit(solution)/shard_map/ppermute | solution.py:19
  108.5 1.3 collective-permute-start.7
  109.8 4.1 pad_maximum_fusion
  113.9 0.7 concatenate.78
  114.6 31.8 %gather_fusion = bf16[1536,64,128]{2,1,0:T(8,128)(2,1)} fusion(bf16[193,64,128]{2,1,0:T(8,128)(2,1)S(1)} %concatenate.78, s32[2048]{0:T(1024)S(1)} %pad_clamp_fusion), kind=kCustom, calls=%fused_computation | custom fusion | bytes 50337792 | tf_op jit(solution)/shard_map/gather | solution.py:73
  146.4 16.1 %fusion = bf16[64,64,128]{2,1,0:T(8,128)(2,1)S(1)} fusion(bf16[64,64,128]{2,1,0:T(8,128)(2,1)} %bitcast.99, f32[64,64,64]{2,1,0:T(8,128)} %get-tuple-element.9, f32[64,64,64]{2,1,0:T(8,128)} %get-tuple-element.8, bf16[64,64,1536]{2,1,0:T(8,128)(2,1)} %param.5, bf16[64,1536,128]{2,1,0:T(8,128)(2,1)} %bitcast.96, bf16[64,128,64]{1,2,0:T(8,128)(2,1)} %get-tuple-element.29, ...), kind=kOutput, calls=%fused_computation.13 | convolution fusion | flops 1615331328 | bytes 42991624 | tf_op jit(solution)/shard_map/bij,bjc->bic/dot_general | solution.py:74
  162.5 0.4 slice_negate_fusion.9
  163.0 3.0 slice.127
  166.0 3.1 fusion.72
  169.1 4.2 collective-permute-start.2
  173.3 1.5 collective-permute-start.3
  174.8 2.8 slice.117
  177.6 1.9 slice_negate_fusion.1
  179.5 2.0 slice_negate_fusion.4
  181.5 4.1 pad_maximum_fusion.3
  185.7 0.7 concatenate.94
  186.4 31.9 %gather_fusion.3 = bf16[1536,64,128]{2,1,0:T(8,128)(2,1)} fusion(bf16[193,64,128]{2,1,0:T(8,128)(2,1)S(1)} %concatenate.94, s32[2048]{0:T(1024)S(1)} %pad_clamp_fusion), kind=kCustom, calls=%fused_computation.3 | custom fusion | bytes 50337792 | tf_op jit(solution)/shard_map/gather | solution.py:73
  218.3 16.1 %fusion.3 = bf16[64,64,128]{2,1,0:T(8,128)(2,1)S(1)} fusion(bf16[64,64,128]{2,1,0:T(8,128)(2,1)} %bitcast.100, f32[64,64,64]{2,1,0:T(8,128)} %slice.127, f32[64,64,64]{2,1,0:T(8,128)} %slice_negate_fusion.1, bf16[64,64,1536]{2,1,0:T(8,128)(2,1)} %param.5, bf16[64,1536,128]{2,1,0:T(8,128)(2,1)} %bitcast.94, bf16[64,64,128]{2,1,0:T(8,128)(2,1)} %get-tuple-element.27, ...), kind=kOutput, calls=%fused_computation.16 | convolution fusion | flops 1615331328 | bytes 42991624 | tf_op jit(solution)/shard_map/bij,bjc->bic/dot_general | solution.py:74
  234.4 0.4 slice_negate_fusion.6
  234.8 1.1 copy-done.12
  236.0 2.1 fusion.36
  238.1 0.2 bitcast_convert_fusion
  238.3 2.7 slice_negate_fusion
  241.0 4.6 pad_maximum_fusion.1
  245.6 0.7 concatenate.83
  246.3 31.9 %gather_fusion.1 = bf16[1536,64,128]{2,1,0:T(8,128)(2,1)} fusion(bf16[193,64,128]{2,1,0:T(8,128)(2,1)S(1)} %concatenate.83, s32[2048]{0:T(1024)S(1)} %pad_clamp_fusion), kind=kCustom, calls=%fused_computation.1 | custom fusion | bytes 50337792 | tf_op jit(solution)/shard_map/gather | solution.py:73
  278.2 16.4 %fusion.1 = bf16[64,64,128]{2,1,0:T(8,128)(2,1)S(1)} fusion(bf16[64,64,128]{2,1,0:T(8,128)(2,1)} %bitcast.101, f32[64,64,64]{2,1,0:T(8,128)} %slice.117, f32[64,64,64]{2,1,0:T(8,128)} %slice_negate_fusion.4, bf16[64,64,1536]{2,1,0:T(8,128)(2,1)} %param.5, bf16[64,1536,128]{2,1,0:T(8,128)(2,1)} %bitcast.93, bf16[64,64,128]{2,1,0:T(8,128)(2,1)} %get-tuple-element.31, ...), kind=kOutput, calls=%fused_computation.14 | convolution fusion | flops 1615331328 | bytes 42991624 | tf_op jit(solution)/shard_map/bij,bjc->bic/dot_general | solution.py:74
  294.6 0.4 slice_negate_fusion.8
  295.0 1.1 copy-done.13
  296.2 2.1 fusion.38
  298.3 0.2 bitcast_convert_fusion.2
  298.5 0.7 slice_negate_fusion.3
  299.2 0.9 copy-done.14
  300.1 0.6 copy-done.15
  300.8 1.1 pad_maximum_fusion.4
  301.9 0.4 copy-done.3
  302.3 6.2 %add_convert_fusion = bf16[8,4096,128]{2,1,0:T(8,128)(2,1)} fusion(f32[4096,128]{1,0:T(8,128)S(1)} %get-tuple-element.37, f32[8]{0:T(128)S(1)} %copy-done.17, f32[4096,128]{1,0:T(8,128)S(1)} %copy-done.3, f32[8]{0:T(128)S(1)} %copy-done.18, f32[4096,128]{1,0:T(8,128)S(1)} %get-tuple-element.36, f32[8]{0:T(128)S(1)} %copy-done.19, ...), kind=kLoop, calls=%fused_computation.4 | loop fusion | flops 33554432 | bytes 16777344 | tf_op jit(solution)/shard_map/convert_element_type | solution.py:94
  308.6 148.0 %reduce-scatter.2.cloned.1.call-done = bf16[2,4096,128]{2,1,0:T(8,128)(2,1)} async-done(((bf16[8,4096,128]{2,1,0:T(8,128)(2,1)}), bf16[2,4096,128]{2,1,0:T(8,128)(2,1)}) %reduce-scatter.2.cloned.1.call-update) | async-done | bytes 2097168 | tf_op jit(solution)/shard_map/reduce_scatter | solution.py:95
  456.6 3.1 fusion.49
  459.7 2.3 convert_element_type.138
  462.0 51.4 %all-reduce.6.cloned.1.call-done = bf16[2,128,128]{1,2,0:T(8,128)(2,1)} async-done(((bf16[2,128,128]{1,2,0:T(8,128)(2,1)}), bf16[2,128,128]{1,2,0:T(8,128)(2,1)}) %all-reduce.6.cloned.1.call-update) | async-done | bytes 65552 | tf_op jit(solution)/shard_map/psum | solution.py:103
  513.4 1.6 copy.11
  (50 shorter events, 0.2 us)
Async XLA Ops:
  7.2 449.4 %reduce-scatter.2.cloned.1.call-start = ((), (), s32[]{:S(2)}) async-start(), calls=%async_computation.1 | async-start | bytes 10485760 | tf_op jit(solution)/shard_map/reduce_scatter | solution.py:95
  7.2 2.2 copy-start
  7.2 2.5 copy-start.9
  10.5 21.1 %copy-start.5 = (bf16[64,128,64]{1,2,0:T(8,128)(2,1)}, bf16[64,128,64]{1,2,0:T(8,128)(2,1)S(1)}, u32[]{:S(2)}) copy-start(bf16[64,128,64]{1,2,0:T(8,128)(2,1)S(1)} %get-tuple-element.25) | copy-start | bytes 3145732
  10.5 14.0 %copy-start.16 = (s32[64,24]{0,1:T(8,128)S(1)}, s32[64,24]{0,1:T(8,128)}, u32[]{:S(2)}) copy-start(s32[64,24]{0,1:T(8,128)} %param.6) | copy-start | bytes 18436
  10.5 14.0 %copy-start.21 = (s32[64]{0:T(128)S(1)}, s32[64]{0:T(128)}, u32[]{:S(2)}) copy-start(s32[64]{0:T(128)} %param.7) | copy-start | bytes 772
  10.5 21.0 %collective-permute-start.4 = (bf16[4096,128]{1,0:T(8,128)(2,1)S(1)}, bf16[4096,128]{1,0:T(8,128)(2,1)}, u32[]{:S(2)}, u32[]{:S(2)}) collective-permute-start(bf16[4096,128]{1,0:T(8,128)(2,1)S(1)} %bitcast.104), channel_id=1, source_target_pairs={{0,1},{1,2},{2,3},{3,4},{4,5},{5,6},{6,7},{8,9},{9,10},{10,11},{11... | collective-permute-start | bytes 3145736 | tf_op jit(solution)/shard_map/ppermute | solution.py:19
  14.1 17.5 %collective-permute-start.5 = (bf16[4096,128]{1,0:T(8,128)(2,1)S(1)}, bf16[4096,128]{1,0:T(8,128)(2,1)}, u32[]{:S(2)}, u32[]{:S(2)}) collective-permute-start(bf16[4096,128]{1,0:T(8,128)(2,1)S(1)} %bitcast.105), channel_id=1, source_target_pairs={{1,0},{2,1},{3,2},{4,3},{5,4},{6,5},{7,6},{9,8},{10,9},{11,10},{12... | collective-permute-start | bytes 3145736 | tf_op jit(solution)/shard_map/ppermute | solution.py:20
  17.8 91.9 %collective-permute-start = (bf16[4096,128]{1,0:T(8,128)(2,1)}, bf16[4096,128]{1,0:T(8,128)(2,1)}, u32[]{:S(2)}, u32[]{:S(2)}) collective-permute-start(bf16[4096,128]{1,0:T(8,128)(2,1)} %bitcast.3), channel_id=1, source_target_pairs={{0,1},{1,2},{2,3},{3,4},{4,5},{5,6},{6,7},{8,9},{9,10},{10,11},{11... | collective-permute-start | bytes 3145736 | tf_op jit(solution)/shard_map/ppermute | solution.py:19
  22.9 86.9 %collective-permute-start.1 = (bf16[4096,128]{1,0:T(8,128)(2,1)}, bf16[4096,128]{1,0:T(8,128)(2,1)}, u32[]{:S(2)}, u32[]{:S(2)}) collective-permute-start(bf16[4096,128]{1,0:T(8,128)(2,1)} %bitcast.3), channel_id=1, source_target_pairs={{1,0},{2,1},{3,2},{4,3},{5,4},{6,5},{7,6},{9,8},{10,9},{11,10},{12... | collective-permute-start | bytes 3145736 | tf_op jit(solution)/shard_map/ppermute | solution.py:20
  25.9 2.8 copy-start.4
  89.4 1.2 copy-start.6
  89.4 1.9 copy-start.10
  93.9 87.6 %collective-permute-start.6 = (bf16[4096,128]{1,0:T(8,128)(2,1)}, bf16[4096,128]{1,0:T(8,128)(2,1)}, u32[]{:S(2)}, u32[]{:S(2)}) collective-permute-start(bf16[4096,128]{1,0:T(8,128)(2,1)} %bitcast.24), channel_id=1, source_target_pairs={{0,1},{1,2},{2,3},{3,4},{4,5},{5,6},{6,7},{8,9},{9,10},{10,11},{11... | collective-permute-start | bytes 3145736 | tf_op jit(solution)/shard_map/ppermute | solution.py:19
  108.5 73.0 %collective-permute-start.7 = (bf16[4096,128]{1,0:T(8,128)(2,1)}, bf16[4096,128]{1,0:T(8,128)(2,1)}, u32[]{:S(2)}, u32[]{:S(2)}) collective-permute-start(bf16[4096,128]{1,0:T(8,128)(2,1)} %bitcast.24), channel_id=1, source_target_pairs={{1,0},{2,1},{3,2},{4,3},{5,4},{6,5},{7,6},{9,8},{10,9},{11,10},{12... | collective-permute-start | bytes 3145736 | tf_op jit(solution)/shard_map/ppermute | solution.py:20
  163.0 3.0 copy-start.11
  169.1 8.5 %copy-start.8 = (f32[64,64,128]{2,1,0:T(8,128)S(1)}, f32[64,64,128]{2,1,0:T(8,128)}, u32[]{:S(2)}) copy-start(f32[64,64,128]{2,1,0:T(8,128)} %get-tuple-element.26) | copy-start | bytes 6291460
  169.1 71.9 %collective-permute-start.2 = (bf16[4096,128]{1,0:T(8,128)(2,1)}, bf16[4096,128]{1,0:T(8,128)(2,1)}, u32[]{:S(2)}, u32[]{:S(2)}) collective-permute-start(bf16[4096,128]{1,0:T(8,128)(2,1)} %bitcast.9), channel_id=1, source_target_pairs={{0,1},{1,2},{2,3},{3,4},{4,5},{5,6},{6,7},{8,9},{9,10},{10,11},{11... | collective-permute-start | bytes 3145736 | tf_op jit(solution)/shard_map/ppermute | solution.py:19
  173.3 67.7 %collective-permute-start.3 = (bf16[4096,128]{1,0:T(8,128)(2,1)}, bf16[4096,128]{1,0:T(8,128)(2,1)}, u32[]{:S(2)}, u32[]{:S(2)}) collective-permute-start(bf16[4096,128]{1,0:T(8,128)(2,1)} %bitcast.9), channel_id=1, source_target_pairs={{1,0},{2,1},{3,2},{4,3},{5,4},{6,5},{7,6},{9,8},{10,9},{11,10},{12... | collective-permute-start | bytes 3145736 | tf_op jit(solution)/shard_map/ppermute | solution.py:20
  234.4 1.6 copy-start.12
  238.3 2.7 copy-start.2
  294.6 1.6 copy-start.13
  298.5 1.6 copy-start.14
  298.5 2.2 copy-start.15
  300.7 1.6 copy-start.3
  300.7 1.6 copy-start.17
  300.7 1.6 copy-start.18
  300.7 1.6 copy-start.19
  300.7 1.6 copy-start.20
  308.5 148.0 %copy-start.1 = (bf16[4096,128]{1,0:T(8,128)(2,1)S(1)}, bf16[4096,128]{1,0:T(8,128)(2,1)}, u32[]{:S(2)}) copy-start(bf16[4096,128]{1,0:T(8,128)(2,1)} %param.9) | copy-start | bytes 3145732
  308.6 204.8 %all-reduce.6.cloned.1.call-start = ((), (), s32[]{:S(2)}) async-start(), calls=%async_computation.2 | async-start | bytes 131072 | tf_op jit(solution)/shard_map/psum | solution.py:103
  456.6 3.2 copy-start.7
Sparse Core Ops, SparseCore 0:
  308.7 147.8 reduce-scatter.1
  460.2 53.1 all-reduce.5
where the time goes:
time: 526 us; the launch traced here: 522 us
  waiting for transfers between devices  199 us (38%)
  local copies, waits for them, and re-layouts  144 us (27%)
  matrix products  81 us (15%)
  other arithmetic  49.8 us (9%)
  starting transfers between devices  32.8 us (6%)
  between operations  15 us (3%)
    reduce_scatter x1, waiting for transfers between devices, shards(): lax.psum_scatter(held.astype(jnp.float32).astype(jnp.bfloat16), 'quad', s...  148 us
    gather x4, local copies, waits for them, and re-layouts, shards(): stacked[local_index].reshape(row_blocks, slots * block_size, width)  128 us
    dot_general x4, matrix products, shards(): jnp.einsum('bij,bjc->bic', hamiltonian, gathered, preferred_element_type=...  64.9 us
    psum x1, waiting for transfers between devices, shards(): lax.psum(local_blocks.astype(jnp.bfloat16), 'row').astype(jnp.float32)  51.4 us
    ppermute x4, starting transfers between devices, extended_2(): before = lax.ppermute(last, axis, up)  27.4 us
    concatenate x4, other arithmetic, extended_2(): x = jnp.concatenate([before, x, after], axis=dim)  21.8 us
    neg x11, other arithmetic, rotate(): -values[..., half_cols:]  16.8 us
    dot_general x6, matrix products, precondition(): jnp.einsum('bij,bjc->bic', blocks_pre, stacked, preferred_element_type=jn...  13.1 us
  transfers between devices with their start and end apart: 10, of which 2 were waited for; matrix products, arithmetic and copies ran while one was open for 38% of the time, Pallas kernels for 0%

commit v1 on v0

v1 whole, which is shorter than its diff:
```python
import functools
import math

import jax
import jax.numpy as jnp
from jax import lax
from jax.experimental import pallas as pl
from jax.experimental.pallas import tpu as pltpu
from jax.sharding import PartitionSpec as P

ITERS = 2
MOMENTS = 8
CHUNKS = 2
TILE = 8
VMEM_LIMIT = 48 * 1024 * 1024
F32 = jnp.float32
BF16 = jnp.bfloat16


def rotated(values, h):
    width = values.shape[1]
    lane = lax.broadcasted_iota(jnp.int32, values.shape, 1)
    first = (lane // h) % 2 == 0
    ahead = pltpu.roll(values, width - h, 1)
    behind = pltpu.roll(values, h, 1)
    return jnp.where(first, -ahead, behind)


def apply_inverse(pre_ref, t, resid, h):
    per_quad = pre_ref.shape[0]
    bs, width = resid.shape
    stacked = jnp.concatenate([resid.astype(BF16), rotated(resid, h).astype(BF16)], axis=0)
    blocks = jnp.concatenate([pre_ref[q, t] for q in range(per_quad)], axis=0)
    both = jnp.dot(blocks, stacked, preferred_element_type=F32)
    lane = lax.broadcasted_iota(jnp.int32, resid.shape, 1)
    out = both[:bs]
    for q in range(1, per_quad):
        out = jnp.where(lane // (2 * h) == q, both[q * bs : (q + 1) * bs], out)
    return out


def init_kernel(h, pre_ref, rhs_ref, out_ref):
    tile, bs = out_ref.shape[0], out_ref.shape[1]
    for t in range(tile):
        out_ref[t] = apply_inverse(pre_ref, t, rhs_ref[t].astype(F32), h).astype(BF16)


def sweep_kernel(
    h, last, index_ref, ham_ref, pre_ref, rhs_ref, full_ref, coef_ref, before_ref, own_ref, after_ref, *rest
):
    if last:
        out_ref, terms_ref, held, sems = rest
    else:
        out_ref, held, sems = rest
    tile, bs, width = out_ref.shape
    nb = own_ref.shape[0]
    slots = ham_ref.shape[2] // bs
    step = pl.program_id(0)

    @pl.when(step == 0)
    def _():
        copies = [
            pltpu.make_async_copy(src, held.at[pl.ds(k * nb, nb)], sems.at[k])
            for k, src in enumerate((before_ref, own_ref, after_ref))
        ]
        for copy in copies:
            copy.start()
        held[3 * nb] = jnp.zeros((bs, width), BF16)
        if last:
            terms_ref[...] = jnp.zeros_like(terms_ref)
        for copy in copies:
            copy.wait()

    zreal = coef_ref[0:1, :]
    zimag = coef_ref[1:2, :]
    group = max(1, 256 // bs)
    for t in range(tile):
        b = step * tile + t
        product = None
        for s in range(0, slots, group):
            wide = min(group, slots - s)
            gathered = jnp.concatenate([held[index_ref[b, s + k]] for k in range(wide)], axis=0)
            term = jnp.dot(
                ham_ref[t, :, s * bs : (s + wide) * bs], gathered, preferred_element_type=F32
            )
            product = term if product is None else product + term
        current = held[nb + b].astype(F32)
        shifted = zreal * current + zimag * rotated(current, h)
        resid = (rhs_ref[t].astype(F32) - (shifted - product)).astype(BF16).astype(F32)
        out_ref[t] = (current + apply_inverse(pre_ref, t, resid, h)).astype(BF16)
    if last:
        terms_ref[...] += lax.dot_general(
            full_ref[...].reshape(tile * bs, full_ref.shape[2]),
            out_ref[...].reshape(tile * bs, width),
            (((0,), (0,)), ((), ())),
            preferred_element_type=F32,
        )


def mix_kernel(own_ref, pair_ref, mix_ref, out_ref):
    pack = jnp.concatenate([own_ref[...], pair_ref[...]], axis=1)
    wide = jnp.dot(pack, mix_ref[0], preferred_element_type=F32)
    out_ref[...] = (wide + jnp.dot(pack, mix_ref[1], preferred_element_type=F32)).astype(BF16)


def final_kernel(chunks, others, per_device, *refs):
    own, pair = refs[:chunks], refs[chunks : 2 * chunks]
    got = refs[2 * chunks : (2 + others) * chunks]
    mix_ref, place_ref, out_ref = refs[(2 + others) * chunks :]
    total = None
    for c in range(chunks):
        pack = jnp.concatenate([own[c][...], pair[c][...]], axis=1)
        part = jnp.dot(pack, mix_ref[c, 0], preferred_element_type=F32)
        part = part + jnp.dot(pack, mix_ref[c, 1], preferred_element_type=F32)
        for k in range(others):
            part = part + jnp.dot(
                got[c * others + k][...], place_ref[c], preferred_element_type=F32
            )
        total = part if total is None else total + part
    width = total.shape[1] // per_device
    for a in range(per_device):
        out_ref[a] = total[:, a * width : (a + 1) * width]


def split_two(values):
    high = values.astype(BF16)
    low = (values - high.astype(F32)).astype(BF16)
    return jnp.stack([high, low])


def shards(hamiltonian, columns, counts, precond, rhs):
    nb, bs, _ = hamiltonian.shape
    slots = columns.shape[1]
    width = rhs.shape[1]
    half = width // 2
    per_quad = precond.shape[0]
    quad_count = lax.axis_size("quad")
    row_count = lax.axis_size("row")
    quads_total = per_quad * quad_count
    per_device = MOMENTS // quad_count
    rows = nb * bs
    row_index = lax.axis_index("row")
    quad_index = lax.axis_index("quad")
    h = half // CHUNKS
    wide = per_quad * 2 * h
    tile = TILE
    params = pltpu.CompilerParams(vmem_limit_bytes=VMEM_LIMIT)

    first_block = (row_index - 1) * nb
    live = jnp.arange(slots)[None, :] < counts[:, None]
    index = jnp.where(live, columns - first_block, 3 * nb).astype(jnp.int32)

    def theta_of(j):
        return 2.0 * jnp.pi * (j.astype(F32) + 0.5) / quads_total

    points = quad_index * per_quad + jnp.arange(per_quad)
    lane_theta = jnp.repeat(theta_of(points), 2 * h)
    coefs = jnp.concatenate(
        [jnp.cos(lane_theta)[None], jnp.sin(lane_theta)[None], jnp.zeros((6, wide), F32)], axis=0
    )

    partner = quad_index + 1 - 2 * (quad_index % 2)
    pairs = quad_count // 2
    my_pair, my_side = quad_index // 2, quad_index % 2
    owners = [quad_index] + [
        ((my_pair + d) % pairs) * 2 + (1 - my_side) for d in range(1, pairs)
    ]
    moment_of = jnp.stack(owners)[:, None] * per_device + jnp.arange(per_device)[None, :]
    sources = jnp.stack([quad_index, partner])[:, None] * per_quad + jnp.arange(per_quad)[None, :]
    phase = theta_of(sources)[:, :, None, None] * (moment_of.astype(F32) + 1.0)[None, None]
    cos, sin = jnp.cos(phase) / quads_total, jnp.sin(phase) / quads_total
    coef = jnp.stack(
        [jnp.stack([cos, sin], axis=-1), jnp.stack([-sin, cos], axis=-1)], axis=2
    )
    send_mix = jnp.einsum("rqptak,lm->trqplakm", coef[:, :, :, 1:], jnp.eye(h, dtype=F32))
    send_mix = send_mix.reshape(pairs - 1, 2 * wide, per_device * 2 * h)
    place = jnp.stack([jnp.eye(half, dtype=F32)[c * h : (c + 1) * h] for c in range(CHUNKS)])
    keep_mix = jnp.einsum("rqpak,clm->crqplakm", coef[:, :, :, 0], place)
    keep_mix = keep_mix.reshape(CHUNKS, 2 * wide, per_device * width)
    both_eye = jnp.eye(per_device * 2, dtype=F32).reshape(per_device, 2, per_device, 2)
    place_mix = jnp.einsum("apbk,clm->caplbkm", both_eye, place)
    place_mix = place_mix.reshape(CHUNKS, per_device * 2 * h, per_device * width).astype(BF16)
    send_mix = jnp.swapaxes(split_two(send_mix), 0, 1)
    keep_mix = jnp.swapaxes(split_two(keep_mix), 0, 1)

    rhs_full = rhs.reshape(nb, bs, width)
    rhs_parts = rhs.reshape(rows, 2, CHUNKS, h)
    up = [(i, i + 1) for i in range(row_count - 1)]
    down = [(i + 1, i) for i in range(row_count - 1)]
    swaps = [(i, i + 1 - 2 * (i % 2)) for i in range(quad_count)]

    grid = (nb // tile,)
    pre_spec = pl.BlockSpec((per_quad, tile, bs, 2 * bs), lambda i, *_: (0, i, 0, 0))
    field_spec = pl.BlockSpec((tile, bs, wide), lambda i, *_: (i, 0, 0))
    any_spec = pl.BlockSpec(memory_space=pl.ANY)
    field = jax.ShapeDtypeStruct((nb, bs, wide), BF16)

    def initial(chunk_rhs):
        return pl.pallas_call(
            functools.partial(init_kernel, h),
            grid=grid,
            in_specs=[pre_spec, field_spec],
            out_specs=field_spec,
            out_shape=field,
            compiler_params=params,
            cost_estimate=pl.CostEstimate(
                flops=4 * rows * bs * wide * per_quad, bytes_accessed=4 * rows * wide + 2 * precond.size,
                transcendentals=0,
            ),
            name="initial",
        )(precond, chunk_rhs)

    def sweep(chunk_rhs, before, own, after, last):
        out_specs, out_shape = field_spec, field
        if last:
            out_specs = [field_spec, pl.BlockSpec((width, wide), lambda i, *_: (0, 0))]
            out_shape = [field, jax.ShapeDtypeStruct((width, wide), F32)]
        return pl.pallas_call(
            functools.partial(sweep_kernel, h, last),
            grid_spec=pltpu.PrefetchScalarGridSpec(
                num_scalar_prefetch=1,
                grid=grid,
                in_specs=[
                    pl.BlockSpec((tile, bs, slots * bs), lambda i, *_: (i, 0, 0)),
                    pre_spec,
                    field_spec,
                    pl.BlockSpec((tile, bs, width), lambda i, *_: (i, 0, 0)),
                    pl.BlockSpec((8, wide), lambda i, *_: (0, 0)),
                    any_spec,
                    any_spec,
                    any_spec,
                ],
                out_specs=out_specs,
                scratch_shapes=[
                    pltpu.VMEM((3 * nb + 1, bs, wide), BF16),
                    pltpu.SemaphoreType.DMA((3,)),
                ],
            ),
            out_shape=out_shape,
            compiler_params=params,
            cost_estimate=pl.CostEstimate(
                flops=2 * hamiltonian.size * wide, bytes_accessed=2 * hamiltonian.size + 10 * rows * wide,
                transcendentals=0,
            ),
            name="sweep",
        )(index, hamiltonian, precond, chunk_rhs, rhs_full, coefs, before, own, after)

    tall = 512
    flat_spec = pl.BlockSpec((tall, wide), lambda i: (i, 0))
    sent_spec = pl.BlockSpec((tall, per_device * 2 * h), lambda i: (i, 0))

    def whole_spec(array):
        return pl.BlockSpec(array.shape, lambda i: (0,) * array.ndim)

    def mixed(own, pair, mix):
        return pl.pallas_call(
            mix_kernel,
            grid=(rows // tall,),
            in_specs=[flat_spec, flat_spec, whole_spec(mix)],
            out_specs=sent_spec,
            out_shape=jax.ShapeDtypeStruct((rows, per_device * 2 * h), BF16),
            compiler_params=params,
            cost_estimate=pl.CostEstimate(
                flops=4 * rows * mix.shape[1] * mix.shape[2], bytes_accessed=6 * rows * wide, transcendentals=0
            ),
            name="mixed",
        )(own, pair, mix)

    parts = [
        jnp.concatenate([rhs_parts[:, p, c] for _ in range(per_quad) for p in range(2)], axis=1)
        .reshape(nb, bs, wide)
        for c in range(CHUNKS)
    ]
    finals, partners, received, terms = [], [], [], []
    for c in range(CHUNKS):
        iterate = initial(parts[c])
        term = None
        for sweep_no in range(ITERS):
            before = lax.ppermute(iterate, "row", up)
            after = lax.ppermute(iterate, "row", down)
            last = sweep_no == ITERS - 1
            iterate = sweep(parts[c], before, iterate, after, last)
            if last:
                iterate, term = iterate
        own = iterate.reshape(rows, wide)
        pair = lax.ppermute(own, "quad", swaps)
        finals.append(own)
        partners.append(pair)
        terms.append(term.reshape(width, per_quad, 2, h))
        for d in range(1, pairs):
            route = [
                (p * 2 + s, ((p + d) % pairs) * 2 + 1 - s) for p in range(pairs) for s in range(2)
            ]
            received.append(lax.ppermute(mixed(own, pair, send_mix[d - 1]), "quad", route))

    scale = 1.0 / math.sqrt(rows * row_count)
    orders = jnp.arange(MOMENTS).astype(F32) + 1.0
    terms = jnp.stack(terms, axis=3).reshape(width, per_quad, 2, half)
    own_phase = orders[:, None] * theta_of(points)[None, :]
    own_cos = (jnp.cos(own_phase) * (scale / quads_total))[:, None, :, None]
    own_sin = (jnp.sin(own_phase) * (scale / quads_total))[:, None, :, None]
    re, im = terms[None, :, :, 0], terms[None, :, :, 1]
    block_re = jnp.sum(own_cos * re - own_sin * im, axis=2)
    block_im = jnp.sum(own_cos * im + own_sin * re, axis=2)
    local_blocks = jnp.concatenate([block_re, block_im], axis=-1).astype(BF16)
    all_blocks = lax.psum(local_blocks, ("quad", "row"))
    blocks_out = lax.dynamic_slice_in_dim(all_blocks, quad_index * per_device, per_device, 0).astype(F32)

    moments_out = pl.pallas_call(
        functools.partial(final_kernel, CHUNKS, pairs - 1, per_device),
        grid=(rows // tall,),
        in_specs=[flat_spec] * (2 * CHUNKS)
        + [sent_spec] * len(received)
        + [whole_spec(keep_mix), whole_spec(place_mix)],
        out_specs=pl.BlockSpec((per_device, tall, width), lambda i: (0, i, 0)),
        out_shape=jax.ShapeDtypeStruct((per_device, rows, width), F32),
        compiler_params=params,
        name="final",
    )(*finals, *partners, *received, keep_mix, place_mix)
    return (moments_out, blocks_out)


def solution(mesh):
    return jax.shard_map(
        shards,
        mesh=mesh,
        in_specs=(
            P("row", None, None),
            P("row", None),
            P("row"),
            P("quad", "row", None, None),
            P("row", None),
        ),
        out_specs=(P("quad", "row", None), P("quad", None, None)),
        check_vma=False,
    )
```

time: 526 us -> 380 us (0.72)
  local copies, waits for them, and re-layouts: 144 us -> 13 us
  Pallas kernels: 0 us -> 126 us
  matrix products: 81 us -> 0 us
  other arithmetic: 49.8 us -> 11.2 us
  waiting for transfers between devices: 199 us -> 183 us
    reduce_scatter x1 -> x0, waiting for transfers between devices: 148 us -> none  [shards(): lax.psum_scatter(held.astype(jnp.float32).astype(jnp.bfloat16), 'quad', s...]
    gather x4 -> x0, local copies, waits for them, and re-layouts: 128 us -> none  [shards(): stacked[local_index].reshape(row_blocks, slots * block_size, width)]
    pallas_call x0 -> x9, Pallas kernels: none -> 126 us  [the longest x4 95.8 us: sweep(): pl.pallas_call(functools.partial(sweep_kernel, h, last), grid_spec=pltpu....]
    psum x1, waiting for transfers between devices: 51.4 us -> 172 us  [shards(): all_blocks = lax.psum(local_blocks, ('quad', 'row'))]
    dot_general x11 -> x0, matrix products: 81 us -> none  [the longest x4 64.9 us: shards(): jnp.einsum('bij,bjc->bic', hamiltonian, gathered, preferred_element_type=...]
    neg x11 -> x1, other arithmetic: 16.8 us -> 0.21 us  [shards(): -sin]
    concatenate x5 -> x4, other arithmetic: 23 us -> 6.44 us  [the longest x2 5.63 us: shards(): jnp.concatenate([rhs_parts[:, p, c] for _ in range(per_quad) for p in ran...]
    ppermute x8 -> x12, waiting for transfers between devices: 0.02 us -> 11 us  [the longest x2 10.9 us: shards(): pair = lax.ppermute(own, 'quad', swaps)]
  transfers between devices with their start and end apart: 10 -> 13, of which waited for: 2 -> 2; matrix products, arithmetic and copies ran while one was open for 38% -> 4% of each run, Pallas kernels for 0% -> 30%
where the time goes in v1:
time: 380 us; the launch traced here: 379 us
  waiting for transfers between devices  183 us (48%)
  Pallas kernels  126 us (33%)
  starting transfers between devices  32.1 us (8%)
  between operations  14.4 us (4%)
  local copies, waits for them, and re-layouts  13 us (3%)
  other arithmetic  11.2 us (3%)
    psum x1, waiting for transfers between devices, shards(): all_blocks = lax.psum(local_blocks, ('quad', 'row'))  172 us
    pallas_call x4, Pallas kernels, sweep(): pl.pallas_call(functools.partial(sweep_kernel, h, last), grid_spec=pltpu....  95.8 us
    ppermute x4, starting transfers between devices, shards(): before = lax.ppermute(iterate, 'row', up)  18.4 us
    pallas_call x2, Pallas kernels, mixed(): pl.pallas_call(mix_kernel, grid=(rows // tall,), in_specs=[flat_spec, fla...  12.6 us
    ppermute x2, waiting for transfers between devices, shards(): pair = lax.ppermute(own, 'quad', swaps)  10.9 us
    pallas_call x1, Pallas kernels, shards(): pl.pallas_call(functools.partial(final_kernel, CHUNKS, pairs - 1, per_dev...  8.65 us
    pallas_call x2, Pallas kernels, initial(): pl.pallas_call(functools.partial(init_kernel, h), grid=grid, in_specs=[pr...  8.51 us
  transfers between devices with their start and end apart: 13, of which 2 were waited for; matrix products, arithmetic and copies ran while one was open for 4% of the time, Pallas kernels for 30%

profile of v1, /device:TPU:0, one launch (start us, length us, event | category | flops | bytes accessed | tf_op | source)
XLA Modules:
  0.0 379.0 jit_solution(13171886703505057601)
XLA Ops:
  7.2 0.0 all-reduce.2.cloned.1.call-start
  7.2 1.5 copy.28
  8.7 0.9 fusion.11
  9.6 0.5 copy.30
  10.1 0.0 copy-start
  10.1 2.4 copy.29
  12.5 2.7 pad_maximum_fusion.rhs_ref
  15.2 4.3 %initial.2.own_ref = bf16[64,64,128]{2,1,0:T(8,128)(2,1)} custom-call(bf16[2,64,64,128]{3,2,1,0:T(8,128)(2,1)S(1)} %copy-done, bf16[64,64,128]{2,1,0:T(8,128)(2,1)S(1)} %pad_maximum_fusion.rhs_ref), custom_call_target="tpu_custom_call" | custom-call | flops 268435456 | bytes 4194304 | tf_op jit(solution)/shard_map/initial/pallas_call | solution.py:199
  19.5 1.3 collective-permute-start.1
  20.8 4.0 %collective-permute-start = (bf16[64,64,128]{2,1,0:T(8,128)(2,1)}, bf16[64,64,128]{2,1,0:T(8,128)(2,1)}, u32[]{:S(2)}, u32[]{:S(2)}) collective-permute-start(bf16[64,64,128]{2,1,0:T(8,128)(2,1)} %initial.2.own_ref), channel_id=1, source_target_pairs={{0,1},{1,2},{2,3},{3,4},{4,5},{5,6},{6,7},{8,9},{9,10},{10,11},{11... | collective-permute-start | bytes 3145736 | tf_op jit(solution)/shard_map/ppermute | solution.py:279
  24.8 1.4 copy.31
  26.2 1.3 copy.32
  27.6 2.9 pad_maximum_fusion.1.rhs_ref
  30.5 4.2 %initial.3.own_ref = bf16[64,64,128]{2,1,0:T(8,128)(2,1)} custom-call(bf16[2,64,64,128]{3,2,1,0:T(8,128)(2,1)S(1)} %copy-done, bf16[64,64,128]{2,1,0:T(8,128)(2,1)S(1)} %pad_maximum_fusion.1.rhs_ref), custom_call_target="tpu_custom_call" | custom-call | flops 268435456 | bytes 4194304 | tf_op jit(solution)/shard_map/initial/pallas_call | solution.py:199
  34.7 1.4 collective-permute-start.5
  36.2 5.1 %collective-permute-start.4 = (bf16[64,64,128]{2,1,0:T(8,128)(2,1)}, bf16[64,64,128]{2,1,0:T(8,128)(2,1)}, u32[]{:S(2)}, u32[]{:S(2)}) collective-permute-start(bf16[64,64,128]{2,1,0:T(8,128)(2,1)} %initial.3.own_ref), channel_id=1, source_target_pairs={{0,1},{1,2},{2,3},{3,4},{4,5},{5,6},{6,7},{8,9},{9,10},{10,11},{11... | collective-permute-start | bytes 3145736 | tf_op jit(solution)/shard_map/ppermute | solution.py:279
  41.3 0.1 add_multiply_fusion.1
  41.4 0.1 add_multiply_fusion
  41.5 0.1 convert_add_fusion
  41.6 0.2 fusion.10
  41.8 0.1 broadcast_in_dim.11
  41.9 0.1 cos.32
  42.0 0.1 broadcast_in_dim.12
  42.1 0.1 sin.36
  42.1 0.1 maximum_bitcast_fusion.3
  42.3 0.1 copy.27
  42.4 0.2 multiply_bitcast_fusion.1
  42.6 0.4 reshape.332
  43.0 0.1 pad.26.clone
  43.1 0.1 maximum_maximum_fusion.coef_ref
  43.2 0.1 subtract_select_fusion.index_ref
  43.3 0.0 collective-permute-done.1.after_ref
  43.3 23.4 %sweep.4.own_ref = bf16[64,64,128]{2,1,0:T(8,128)(2,1)} custom-call(s32[64,24]{1,0:T(8,128)S(1)} %subtract_select_fusion.index_ref, bf16[64,64,1536]{2,1,0:T(8,128)(2,1)} %ham_ref.7, bf16[2,64,64,128]{3,2,1,0:T(8,128)(2,1)} %pre_ref.11, bf16[64,64,128]{2,1,0:T(8,128)(2,1)S(1)} %copy-done.3, bf16[64,64,128]{2,1,0:T(8,128)(2,1)S(1)} %bitcast.44, ...), custom_call_target="tpu_custom_call" | custom-call | flops 1610612736 | bytes 17825792 | tf_op jit(solution)/shard_map/sweep/pallas_call | solution.py:218
  66.7 1.3 collective-permute-start.3
  68.0 5.0 %collective-permute-start.2 = (bf16[64,64,128]{2,1,0:T(8,128)(2,1)}, bf16[64,64,128]{2,1,0:T(8,128)(2,1)}, u32[]{:S(2)}, u32[]{:S(2)}) collective-permute-start(bf16[64,64,128]{2,1,0:T(8,128)(2,1)} %sweep.4.own_ref), channel_id=1, source_target_pairs={{0,1},{1,2},{2,3},{3,4},{4,5},{5,6},{6,7},{8,9},{9,10},{10,11},{11... | collective-permute-start | bytes 3145736 | tf_op jit(solution)/shard_map/ppermute | solution.py:279
  73.0 23.4 %sweep.6.own_ref = bf16[64,64,128]{2,1,0:T(8,128)(2,1)} custom-call(s32[64,24]{1,0:T(8,128)S(1)} %subtract_select_fusion.index_ref, bf16[64,64,1536]{2,1,0:T(8,128)(2,1)} %ham_ref.7, bf16[2,64,64,128]{3,2,1,0:T(8,128)(2,1)} %pre_ref.11, bf16[64,64,128]{2,1,0:T(8,128)(2,1)S(1)} %copy-done.5, bf16[64,64,128]{2,1,0:T(8,128)(2,1)S(1)} %bitcast.45, ...), custom_call_target="tpu_custom_call" | custom-call | flops 1610612736 | bytes 17825792 | tf_op jit(solution)/shard_map/sweep/pallas_call | solution.py:218
  96.4 1.3 collective-permute-start.7
  97.7 4.3 %collective-permute-start.6 = (bf16[64,64,128]{2,1,0:T(8,128)(2,1)}, bf16[64,64,128]{2,1,0:T(8,128)(2,1)}, u32[]{:S(2)}, u32[]{:S(2)}) collective-permute-start(bf16[64,64,128]{2,1,0:T(8,128)(2,1)} %sweep.6.own_ref), channel_id=1, source_target_pairs={{0,1},{1,2},{2,3},{3,4},{4,5},{5,6},{6,7},{8,9},{9,10},{10,11},{11... | collective-permute-start | bytes 3145736 | tf_op jit(solution)/shard_map/ppermute | solution.py:279
  102.0 1.5 multiply_bitcast_fusion
  103.5 2.8 reshape.333
  106.3 24.5 %sweep.5 = (bf16[64,64,128]{2,1,0:T(8,128)(2,1)}, f32[128,128]{1,0:T(8,128)S(1)}) custom-call(s32[64,24]{1,0:T(8,128)S(1)} %subtract_select_fusion.index_ref, bf16[64,64,1536]{2,1,0:T(8,128)(2,1)} %ham_ref.7, bf16[2,64,64,128]{3,2,1,0:T(8,128)(2,1)} %pre_ref.11, bf16[64,64,128]{2,1,0:T(8,128)(2,1)S(1)} %copy-done.3, bf16[64,64,128]{2,1,0:T(8,128)(2,1)S(1)} %bitcast.46, ...), custom_call_target="tpu_custom_call" | custom-call | flops 1610612736 | bytes 17825792 | tf_op jit(solution)/shard_map/sweep/pallas_call | solution.py:218
  130.9 1.6 collective-permute-start.8
  132.5 24.5 %sweep.7 = (bf16[64,64,128]{2,1,0:T(8,128)(2,1)}, f32[128,128]{1,0:T(8,128)S(1)}) custom-call(s32[64,24]{1,0:T(8,128)S(1)} %subtract_select_fusion.index_ref, bf16[64,64,1536]{2,1,0:T(8,128)(2,1)} %ham_ref.7, bf16[2,64,64,128]{3,2,1,0:T(8,128)(2,1)} %pre_ref.11, bf16[64,64,128]{2,1,0:T(8,128)(2,1)S(1)} %copy-done.5, bf16[64,64,128]{2,1,0:T(8,128)(2,1)S(1)} %bitcast.47, ...), custom_call_target="tpu_custom_call" | custom-call | flops 1610612736 | bytes 17825792 | tf_op jit(solution)/shard_map/sweep/pallas_call | solution.py:218
  157.0 0.5 collective-permute-start.9
  157.6 0.1 compare_convert_fusion
  157.7 0.1 fusion.6
  157.8 0.8 subtract_convert_fusion
  158.6 0.1 copy.35
  158.7 0.1 copy.36
  158.8 6.3 %mixed.2 = bf16[4096,128]{1,0:T(8,128)(2,1)} custom-call(bf16[4096,128]{1,0:T(8,128)(2,1)} %bitcast.4.own_ref.refs_0_, bf16[4096,128]{1,0:T(8,128)(2,1)S(1)} %collective-permute-done.8.pair_ref.refs_2_, bf16[2,256,128]{2,1,0:T(8,128)(2,1)S(1)} %maximum_bitcast_fusion.1.mix_ref), custom_call_target="tpu_custom_call" | custom-call | flops 536870912 | bytes 3145728 | tf_op jit(solution)/shard_map/mixed/pallas_call | solution.py:256
  165.1 3.6 collective-permute-start.10
  168.7 10.9 %collective-permute-done.9.pair_ref.refs_3_ = bf16[4096,128]{1,0:T(8,128)(2,1)S(1)} collective-permute-done((bf16[4096,128]{1,0:T(8,128)(2,1)}, bf16[4096,128]{1,0:T(8,128)(2,1)S(1)}, u32[]{:S(2)}, u32[]{:S(2)}) %collective-permute-start.9) | collective-permute-done | bytes 1048608 | tf_op jit(solution)/shard_map/ppermute | solution.py:286
  179.6 6.3 %mixed.3 = bf16[4096,128]{1,0:T(8,128)(2,1)} custom-call(bf16[4096,128]{1,0:T(8,128)(2,1)} %bitcast.7.own_ref.refs_1_, bf16[4096,128]{1,0:T(8,128)(2,1)S(1)} %collective-permute-done.9.pair_ref.refs_3_, bf16[2,256,128]{2,1,0:T(8,128)(2,1)S(1)} %maximum_bitcast_fusion.1.mix_ref), custom_call_target="tpu_custom_call" | custom-call | flops 536870912 | bytes 3145728 | tf_op jit(solution)/shard_map/mixed/pallas_call | solution.py:256
  185.9 2.6 collective-permute-start.11
  188.6 0.2 subtract_reduce_fusion
  188.8 0.7 pad_maximum_fusion.2
  189.5 0.0 all-reduce.2.cloned.1.call-update
  189.6 0.2 fusion
  189.8 0.2 convert_element_type.135.refs_7_
  190.0 0.1 maximum_bitcast_fusion.refs_6_
  190.1 171.8 %all-reduce.2.cloned.1.call-done = bf16[8,128,128]{1,2,0:T(8,128)(2,1)} async-done(((bf16[8,128,128]{1,2,0:T(8,128)(2,1)}), bf16[8,128,128]{1,2,0:T(8,128)(2,1)}) %all-reduce.2.cloned.1.call-update) | async-done | bytes 262160 | tf_op jit(solution)/shard_map/psum | solution.py:306
  361.9 0.8 dynamic-slice_convert_fusion
  362.7 0.8 copy.38
  363.5 8.6 %final.1 = f32[2,4096,128]{2,1,0:T(8,128)} custom-call(bf16[4096,128]{1,0:T(8,128)(2,1)} %bitcast.4.own_ref.refs_0_, bf16[4096,128]{1,0:T(8,128)(2,1)} %bitcast.7.own_ref.refs_1_, bf16[4096,128]{1,0:T(8,128)(2,1)S(1)} %collective-permute-done.8.pair_ref.refs_2_, bf16[4096,128]{1,0:T(8,128)(2,1)S(1)} %collective-permute-done.9.pair_ref.refs_3_, ...), custom_call_target="tpu_custom_call" | custom-call | tf_op jit(solution)/shard_map/final/pallas_call | solution.py:309
  (46 shorter events, 0.3 us)
Async XLA Ops:
  7.2 354.7 %all-reduce.2.cloned.1.call-start = ((), (), s32[]{:S(2)}) async-start(), calls=%async_computation | async-start | bytes 524288 | tf_op jit(solution)/shard_map/psum | solution.py:306
  10.1 5.2 %copy-start = (bf16[2,64,64,128]{3,2,1,0:T(8,128)(2,1)S(1)}, bf16[2,64,64,128]{3,2,1,0:T(8,128)(2,1)}, u32[]{:S(2)}) copy-start(bf16[2,64,64,128]{3,2,1,0:T(8,128)(2,1)} %pre_ref.11) | copy-start | bytes 6291460
  15.2 4.3 %copy-start.2 = (bf16[64,64,128]{2,1,0:T(8,128)(2,1)}, bf16[64,64,128]{2,1,0:T(8,128)(2,1)S(1)}, u32[]{:S(2)}) copy-start(bf16[64,64,128]{2,1,0:T(8,128)(2,1)S(1)} %pad_maximum_fusion.rhs_ref) | copy-start | bytes 3145732
  19.5 23.8 %collective-permute-start.1 = (bf16[64,64,128]{2,1,0:T(8,128)(2,1)}, bf16[64,64,128]{2,1,0:T(8,128)(2,1)}, u32[]{:S(2)}, u32[]{:S(2)}) collective-permute-start(bf16[64,64,128]{2,1,0:T(8,128)(2,1)} %initial.2.own_ref), channel_id=1, source_target_pairs={{1,0},{2,1},{3,2},{4,3},{5,4},{6,5},{7,6},{9,8},{10,9},{11,10},{12... | collective-permute-start | bytes 3145736 | tf_op jit(solution)/shard_map/ppermute | solution.py:280
  20.8 22.5 %collective-permute-start = (bf16[64,64,128]{2,1,0:T(8,128)(2,1)}, bf16[64,64,128]{2,1,0:T(8,128)(2,1)}, u32[]{:S(2)}, u32[]{:S(2)}) collective-permute-start(bf16[64,64,128]{2,1,0:T(8,128)(2,1)} %initial.2.own_ref), channel_id=1, source_target_pairs={{0,1},{1,2},{2,3},{3,4},{4,5},{5,6},{6,7},{8,9},{9,10},{10,11},{11... | collective-permute-start | bytes 3145736 | tf_op jit(solution)/shard_map/ppermute | solution.py:279
  30.4 4.3 %copy-start.4 = (bf16[64,64,128]{2,1,0:T(8,128)(2,1)}, bf16[64,64,128]{2,1,0:T(8,128)(2,1)S(1)}, u32[]{:S(2)}) copy-start(bf16[64,64,128]{2,1,0:T(8,128)(2,1)S(1)} %pad_maximum_fusion.1.rhs_ref) | copy-start | bytes 3145732
  30.5 11.8 %copy-start.8 = (s32[64,24]{0,1:T(8,128)S(1)}, s32[64,24]{0,1:T(8,128)}, u32[]{:S(2)}) copy-start(s32[64,24]{0,1:T(8,128)} %param.6) | copy-start | bytes 18436
  30.5 12.7 %copy-start.9 = (s32[64]{0:T(128)S(1)}, s32[64]{0:T(128)}, u32[]{:S(2)}) copy-start(s32[64]{0:T(128)} %param.7) | copy-start | bytes 772
  30.5 12.8 %copy-start.1 = (bf16[4096,128]{1,0:T(8,128)(2,1)S(1)}, bf16[4096,128]{1,0:T(8,128)(2,1)}, u32[]{:S(2)}) copy-start(bf16[4096,128]{1,0:T(8,128)(2,1)} %param.9) | copy-start | bytes 3145732
  34.7 8.6 %copy-start.3 = (bf16[64,64,128]{2,1,0:T(8,128)(2,1)S(1)}, bf16[64,64,128]{2,1,0:T(8,128)(2,1)}, u32[]{:S(2)}) copy-start(bf16[64,64,128]{2,1,0:T(8,128)(2,1)} %copy-done.2) | copy-start | bytes 3145732
  34.7 38.2 %collective-permute-start.5 = (bf16[64,64,128]{2,1,0:T(8,128)(2,1)}, bf16[64,64,128]{2,1,0:T(8,128)(2,1)}, u32[]{:S(2)}, u32[]{:S(2)}) collective-permute-start(bf16[64,64,128]{2,1,0:T(8,128)(2,1)} %initial.3.own_ref), channel_id=1, source_target_pairs={{1,0},{2,1},{3,2},{4,3},{5,4},{6,5},{7,6},{9,8},{10,9},{11,10},{12... | collective-permute-start | bytes 3145736 | tf_op jit(solution)/shard_map/ppermute | solution.py:280
  36.2 36.8 %collective-permute-start.4 = (bf16[64,64,128]{2,1,0:T(8,128)(2,1)}, bf16[64,64,128]{2,1,0:T(8,128)(2,1)}, u32[]{:S(2)}, u32[]{:S(2)}) collective-permute-start(bf16[64,64,128]{2,1,0:T(8,128)(2,1)} %initial.3.own_ref), channel_id=1, source_target_pairs={{0,1},{1,2},{2,3},{3,4},{4,5},{5,6},{6,7},{8,9},{9,10},{10,11},{11... | collective-permute-start | bytes 3145736 | tf_op jit(solution)/shard_map/ppermute | solution.py:279
  43.3 29.7 %copy-start.5 = (bf16[64,64,128]{2,1,0:T(8,128)(2,1)S(1)}, bf16[64,64,128]{2,1,0:T(8,128)(2,1)}, u32[]{:S(2)}) copy-start(bf16[64,64,128]{2,1,0:T(8,128)(2,1)} %copy-done.4) | copy-start | bytes 3145732
  66.7 39.6 %collective-permute-start.3 = (bf16[64,64,128]{2,1,0:T(8,128)(2,1)}, bf16[64,64,128]{2,1,0:T(8,128)(2,1)}, u32[]{:S(2)}, u32[]{:S(2)}) collective-permute-start(bf16[64,64,128]{2,1,0:T(8,128)(2,1)} %sweep.4.own_ref), channel_id=1, source_target_pairs={{1,0},{2,1},{3,2},{4,3},{5,4},{6,5},{7,6},{9,8},{10,9},{11,10},{12... | collective-permute-start | bytes 3145736 | tf_op jit(solution)/shard_map/ppermute | solution.py:280
  68.0 38.3 %collective-permute-start.2 = (bf16[64,64,128]{2,1,0:T(8,128)(2,1)}, bf16[64,64,128]{2,1,0:T(8,128)(2,1)}, u32[]{:S(2)}, u32[]{:S(2)}) collective-permute-start(bf16[64,64,128]{2,1,0:T(8,128)(2,1)} %sweep.4.own_ref), channel_id=1, source_target_pairs={{0,1},{1,2},{2,3},{3,4},{4,5},{5,6},{6,7},{8,9},{9,10},{10,11},{11... | collective-permute-start | bytes 3145736 | tf_op jit(solution)/shard_map/ppermute | solution.py:279
  96.4 36.1 %collective-permute-start.7 = (bf16[64,64,128]{2,1,0:T(8,128)(2,1)}, bf16[64,64,128]{2,1,0:T(8,128)(2,1)}, u32[]{:S(2)}, u32[]{:S(2)}) collective-permute-start(bf16[64,64,128]{2,1,0:T(8,128)(2,1)} %sweep.6.own_ref), channel_id=1, source_target_pairs={{1,0},{2,1},{3,2},{4,3},{5,4},{6,5},{7,6},{9,8},{10,9},{11,10},{12... | collective-permute-start | bytes 3145736 | tf_op jit(solution)/shard_map/ppermute | solution.py:280
  97.7 34.8 %collective-permute-start.6 = (bf16[64,64,128]{2,1,0:T(8,128)(2,1)}, bf16[64,64,128]{2,1,0:T(8,128)(2,1)}, u32[]{:S(2)}, u32[]{:S(2)}) collective-permute-start(bf16[64,64,128]{2,1,0:T(8,128)(2,1)} %sweep.6.own_ref), channel_id=1, source_target_pairs={{0,1},{1,2},{2,3},{3,4},{4,5},{5,6},{6,7},{8,9},{9,10},{10,11},{11... | collective-permute-start | bytes 3145736 | tf_op jit(solution)/shard_map/ppermute | solution.py:279
  130.9 26.9 %copy-start.6 = (f32[1,2,256,256]{3,2,0,1:T(8,128)S(1)}, f32[1,2,256,256]{3,2,0,1:T(8,128)}, u32[]{:S(2)}) copy-start(f32[1,2,256,256]{3,2,0,1:T(8,128)} %reshape.333) | copy-start | bytes 1572868
  130.9 27.9 %collective-permute-start.8 = (bf16[4096,128]{1,0:T(8,128)(2,1)}, bf16[4096,128]{1,0:T(8,128)(2,1)S(1)}, u32[]{:S(2)}, u32[]{:S(2)}) collective-permute-start(bf16[4096,128]{1,0:T(8,128)(2,1)} %bitcast.4.own_ref.refs_0_), channel_id=1, source_target_pairs={{0,8},{8,0},{16,24},{24,16},{1,9},{9,1},{17,25},{25,17},{2,10},{10... | collective-permute-start | bytes 3145736 | tf_op jit(solution)/shard_map/ppermute | solution.py:286
  157.0 22.6 %collective-permute-start.9 = (bf16[4096,128]{1,0:T(8,128)(2,1)}, bf16[4096,128]{1,0:T(8,128)(2,1)S(1)}, u32[]{:S(2)}, u32[]{:S(2)}) collective-permute-start(bf16[4096,128]{1,0:T(8,128)(2,1)} %bitcast.7.own_ref.refs_1_), channel_id=1, source_target_pairs={{0,8},{8,0},{16,24},{24,16},{1,9},{9,1},{17,25},{25,17},{2,10},{10... | collective-permute-start | bytes 3145736 | tf_op jit(solution)/shard_map/ppermute | solution.py:286
  165.1 198.4 %collective-permute-start.10 = (bf16[4096,128]{1,0:T(8,128)(2,1)}, bf16[4096,128]{1,0:T(8,128)(2,1)}, u32[]{:S(2)}, u32[]{:S(2)}) collective-permute-start(bf16[4096,128]{1,0:T(8,128)(2,1)} %mixed.2), channel_id=1, source_target_pairs={{0,24},{8,16},{16,8},{24,0},{1,25},{9,17},{17,9},{25,1},{2,26},{10... | collective-permute-start | bytes 3145736 | tf_op jit(solution)/shard_map/ppermute | solution.py:294
  185.9 4.1 %copy-start.7 = (bf16[1,2,256,256]{3,2,0,1:T(8,128)(2,1)S(1)}, bf16[1,2,256,256]{3,2,0,1:T(8,128)(2,1)}, u32[]{:S(2)}) copy-start(bf16[1,2,256,256]{3,2,0,1:T(8,128)(2,1)} %get-tuple-element.15) | copy-start | bytes 786436
  185.9 177.6 %collective-permute-start.11 = (bf16[4096,128]{1,0:T(8,128)(2,1)}, bf16[4096,128]{1,0:T(8,128)(2,1)}, u32[]{:S(2)}, u32[]{:S(2)}) collective-permute-start(bf16[4096,128]{1,0:T(8,128)(2,1)} %mixed.3), channel_id=1, source_target_pairs={{0,24},{8,16},{16,8},{24,0},{1,25},{9,17},{17,9},{25,1},{2,26},{10... | collective-permute-start | bytes 3145736 | tf_op jit(solution)/shard_map/ppermute | solution.py:294
Sparse Core Ops, SparseCore 0:
  189.7 172.1 all-reduce.1

commit v2 on v1

--- a/solution.py
+++ b/solution.py
@@ -11,8 +11,9 @@
 ITERS = 2
 MOMENTS = 8
 CHUNKS = 2
-TILE = 8
+TILE = 16
 VMEM_LIMIT = 48 * 1024 * 1024
+MESH = pl.DeviceIdType.MESH
 F32 = jnp.float32
 BF16 = jnp.bfloat16
 
@@ -26,32 +27,37 @@
     return jnp.where(first, -ahead, behind)
 
 
-def apply_inverse(pre_ref, t, resid, h):
-    per_quad = pre_ref.shape[0]
-    bs, width = resid.shape
-    stacked = jnp.concatenate([resid.astype(BF16), rotated(resid, h).astype(BF16)], axis=0)
-    blocks = jnp.concatenate([pre_ref[q, t] for q in range(per_quad)], axis=0)
-    both = jnp.dot(blocks, stacked, preferred_element_type=F32)
-    lane = lax.broadcasted_iota(jnp.int32, resid.shape, 1)
-    out = both[:bs]
-    for q in range(1, per_quad):
-        out = jnp.where(lane // (2 * h) == q, both[q * bs : (q + 1) * bs], out)
-    return out
+def apply_inverse(pre_ref, resid, h):
+    per_quad, tile = pre_ref.shape[0], pre_ref.shape[1]
+    _, bs, width = resid.shape
+    turned = rotated(resid.reshape(tile * bs, width), h).astype(BF16)
+    plain = resid.astype(BF16).reshape(tile * bs, width)
+    lane = lax.broadcasted_iota(jnp.int32, (bs, width), 1)
+    outs = []
+    for t in range(tile):
+        own = slice(t * bs, (t + 1) * bs)
+        stacked = jnp.concatenate([plain[own], turned[own]], axis=0)
+        blocks = jnp.concatenate([pre_ref[q, t] for q in range(per_quad)], axis=0)
+        both = jnp.dot(blocks, stacked, preferred_element_type=F32)
+        out = both[:bs]
+        for q in range(1, per_quad):
+            out = jnp.where(lane // (2 * h) == q, both[q * bs : (q + 1) * bs], out)
+        outs.append(out)
+    return outs
 
 
 def init_kernel(h, pre_ref, rhs_ref, out_ref):
-    tile, bs = out_ref.shape[0], out_ref.shape[1]
-    for t in range(tile):
-        out_ref[t] = apply_inverse(pre_ref, t, rhs_ref[t].astype(F32), h).astype(BF16)
+    for t, block in enumerate(apply_inverse(pre_ref, rhs_ref[...].astype(F32), h)):
+        out_ref[t] = block.astype(BF16)
 
 
 def sweep_kernel(
     h, last, index_ref, ham_ref, pre_ref, rhs_ref, full_ref, coef_ref, before_ref, own_ref, after_ref, *rest
 ):
     if last:
-        out_ref, terms_ref, held, sems = rest
+        out_ref, terms_ref, held, product, sems = rest
     else:
-        out_ref, held, sems = rest
+        out_ref, held, product, sems = rest
     tile, bs, width = out_ref.shape
     nb = own_ref.shape[0]
     slots = ham_ref.shape[2] // bs
@@ -73,21 +79,17 @@
 
     zreal = coef_ref[0:1, :]
     zimag = coef_ref[1:2, :]
-    group = max(1, 256 // bs)
     for t in range(tile):
         b = step * tile + t
-        product = None
-        for s in range(0, slots, group):
-            wide = min(group, slots - s)
-            gathered = jnp.concatenate([held[index_ref[b, s + k]] for k in range(wide)], axis=0)
-            term = jnp.dot(
-                ham_ref[t, :, s * bs : (s + wide) * bs], gathered, preferred_element_type=F32
-            )
-            product = term if product is None else product + term
-        current = held[nb + b].astype(F32)
-        shifted = zreal * current + zimag * rotated(current, h)
-        resid = (rhs_ref[t].astype(F32) - (shifted - product)).astype(BF16).astype(F32)
-        out_ref[t] = (current + apply_inverse(pre_ref, t, resid, h)).astype(BF16)
+        gathered = jnp.concatenate([held[index_ref[b, s]] for s in range(slots)], axis=0)
+        product[t] = jnp.dot(ham_ref[t], gathered, preferred_element_type=F32)
+    current = held[pl.ds(nb + step * tile, tile)].astype(F32).reshape(tile * bs, width)
+    shifted = zreal * current + zimag * rotated(current, h)
+    target = rhs_ref[...].astype(F32).reshape(tile * bs, width)
+    resid = (target - (shifted - product[...].reshape(tile * bs, width))).astype(BF16)
+    resid = resid.astype(F32).reshape(tile, bs, width)
+    for t, block in enumerate(apply_inverse(pre_ref, resid, h)):
+        out_ref[t] = (current[t * bs : (t + 1) * bs] + block).astype(BF16)
     if last:
         terms_ref[...] += lax.dot_general(
             full_ref[...].reshape(tile * bs, full_ref.shape[2]),
@@ -120,6 +122,66 @@
     width = total.shape[1] // per_device
     for a in range(per_device):
         out_ref[a] = total[:, a * width : (a + 1) * width]
+
+
+def sum_kernel(rows_n, quads_n, coef_ref, terms_ref, out_ref, parts, mine, quads, held, *sems):
+    me_row, me_quad = lax.axis_index("row"), lax.axis_index("quad")
+    piece = mine.shape[0]
+    per_device, width = held.shape[0], held.shape[2]
+    per_quad = mine.shape[1] // width
+    row_peers = [lax.rem(me_row + d, rows_n) for d in range(1, rows_n)]
+    quad_peers = [lax.rem(me_quad + d, quads_n) for d in range(1, quads_n)]
+
+    barrier = pltpu.get_barrier_semaphore()
+    for peer in row_peers:
+        pl.semaphore_signal(barrier, inc=1, device_id=(me_quad, peer), device_id_type=MESH)
+    for peer in quad_peers:
+        pl.semaphore_signal(barrier, inc=1, device_id=(peer, me_row), device_id_type=MESH)
+    pl.semaphore_wait(barrier, rows_n - 1 + quads_n - 1)
+
+    def send(k, src, dst, peer_quad, peer_row, d):
+        copy = pltpu.make_async_remote_copy(
+            src_ref=src,
+            dst_ref=dst,
+            send_sem=sems[2 * k].at[d],
+            recv_sem=sems[2 * k + 1].at[d],
+            device_id=(peer_quad, peer_row),
+            device_id_type=MESH,
+        )
+        copy.start()
+        return copy
+
+    copies = [
+        send(0, terms_ref.at[pl.ds(pl.multiple_of(peer * piece, piece), piece)], parts.at[d], me_quad, peer, d)
+        for d, peer in enumerate(row_peers)
+    ]
+    total = terms_ref[pl.ds(pl.multiple_of(me_row * piece, piece), piece), :]
+    for d, copy in enumerate(copies):
+        copy.wait()
+        total = total + parts[d]
+    mine[...] = total
+
+    copies = [send(1, mine, quads.at[d], peer, me_row, d) for d, peer in enumerate(quad_peers)]
+    sums = [jnp.zeros((piece, width), F32) for _ in range(per_device)]
+    for d in range(quads_n):
+        if d:
+            copies[d - 1].wait()
+        for q in range(per_quad):
+            part = mine if d == 0 else quads.at[d - 1]
+            value = part[:, q * width : (q + 1) * width]
+            turned = rotated(value, width // 2)
+            for a in range(per_device):
+                at = (d * per_quad + q) * per_device + a
+                sums[a] = sums[a] + coef_ref[0, at] * value + coef_ref[1, at] * turned
+    here = pl.ds(pl.multiple_of(me_row * piece, piece), piece)
+    for a in range(per_device):
+        held[a, here, :] = sums[a]
+    copies = [
+        send(2, held.at[:, here], held.at[:, here], me_quad, peer, d) for d, peer in enumerate(row_peers)
+    ]
+    for copy in copies:
+        copy.wait()
+    out_ref[...] = held[...]
 
 
 def split_two(values):
@@ -233,6 +295,7 @@
                 out_specs=out_specs,
                 scratch_shapes=[
                     pltpu.VMEM((3 * nb + 1, bs, wide), BF16),
+                    pltpu.VMEM((tile, bs, wide), F32),
                     pltpu.SemaphoreType.DMA((3,)),
                 ],
             ),
@@ -294,17 +357,33 @@
             received.append(lax.ppermute(mixed(own, pair, send_mix[d - 1]), "quad", route))
 
     scale = 1.0 / math.sqrt(rows * row_count)
-    orders = jnp.arange(MOMENTS).astype(F32) + 1.0
-    terms = jnp.stack(terms, axis=3).reshape(width, per_quad, 2, half)
-    own_phase = orders[:, None] * theta_of(points)[None, :]
-    own_cos = (jnp.cos(own_phase) * (scale / quads_total))[:, None, :, None]
-    own_sin = (jnp.sin(own_phase) * (scale / quads_total))[:, None, :, None]
-    re, im = terms[None, :, :, 0], terms[None, :, :, 1]
-    block_re = jnp.sum(own_cos * re - own_sin * im, axis=2)
-    block_im = jnp.sum(own_cos * im + own_sin * re, axis=2)
-    local_blocks = jnp.concatenate([block_re, block_im], axis=-1).astype(BF16)
-    all_blocks = lax.psum(local_blocks, ("quad", "row"))
-    blocks_out = lax.dynamic_slice_in_dim(all_blocks, quad_index * per_device, per_device, 0).astype(F32)
+    terms = jnp.stack(terms, axis=3).reshape(width, per_quad * width)
+    order = (quad_index + quad_count - jnp.arange(quad_count)) % quad_count
+    seen = order[:, None, None] * per_quad + jnp.arange(per_quad)[None, :, None]
+    moment = quad_index * per_device + jnp.arange(per_device)[None, None, :]
+    angle = (theta_of(seen) * (moment.astype(F32) + 1.0)).reshape(-1)
+    sum_coef = jnp.stack([jnp.cos(angle), jnp.sin(angle)]) * (scale / quads_total)
+    piece = width // row_count
+    blocks_out = pl.pallas_call(
+        functools.partial(sum_kernel, row_count, quad_count),
+        in_specs=[pl.BlockSpec(memory_space=pltpu.SMEM), pl.BlockSpec(memory_space=pltpu.VMEM)],
+        out_specs=pl.BlockSpec(memory_space=pltpu.VMEM),
+        out_shape=jax.ShapeDtypeStruct((per_device, width, width), F32),
+        scratch_shapes=[
+            pltpu.VMEM((row_count - 1, piece, per_quad * width), F32),
+            pltpu.VMEM((piece, per_quad * width), F32),
+            pltpu.VMEM((quad_count - 1, piece, per_quad * width), F32),
+            pltpu.VMEM((per_device, width, width), F32),
+        ]
+        + [pltpu.SemaphoreType.DMA((row_count - 1,))] * 2
+        + [pltpu.SemaphoreType.DMA((quad_count - 1,))] * 2
+        + [pltpu.SemaphoreType.DMA((row_count - 1,))] * 2,
+        compiler_params=pltpu.CompilerParams(
+            collective_id=0, has_side_effects=True, vmem_limit_bytes=VMEM_LIMIT
+        ),
+        cost_estimate=pl.CostEstimate(flops=0, bytes_accessed=40 * 1024 * 1024, transcendentals=0),
+        name="sum_blocks",
+    )(sum_coef, terms)
 
     moments_out = pl.pallas_call(
         functools.partial(final_kernel, CHUNKS, pairs - 1, per_device),

time: 380 us -> 235 us (0.62)
  waiting for transfers between devices: 183 us -> 24.6 us
  Pallas kernels: 126 us -> 142 us
  between operations: 14.4 us -> 1.14 us
  starting transfers between devices: 32.1 us -> 38.9 us
    psum x1 -> x0, waiting for transfers between devices: 172 us -> none  [shards(): all_blocks = lax.psum(local_blocks, ('quad', 'row'))]
    pallas_call x0 -> x1, Pallas kernels: none -> 72.2 us  [shards(): pl.pallas_call(functools.partial(sum_kernel, row_count, quad_count), in_s...]
    pallas_call x4, Pallas kernels: 95.8 us -> 48.1 us  [sweep(): pl.pallas_call(functools.partial(sweep_kernel, h, last), grid_spec=pltpu....]
    ppermute x2, waiting for transfers between devices: 10.9 us -> 24.6 us  [shards(): pair = lax.ppermute(own, 'quad', swaps)]
    ppermute x4, starting transfers between devices: 18.4 us -> 24 us  [shards(): before = lax.ppermute(iterate, 'row', up)]
    pallas_call x2, Pallas kernels: 12.6 us -> 8.39 us  [mixed(): pl.pallas_call(mix_kernel, grid=(rows // tall,), in_specs=[flat_spec, fla...]
  transfers between devices with their start and end apart: 13 -> 12, of which waited for: 2 -> 2; matrix products, arithmetic and copies ran while one was open for 4% -> 6% of each run, Pallas kernels for 30% -> 56%
where the time goes in v2:
time: 235 us; the launch traced here: 234 us
  Pallas kernels  142 us (60%)
  starting transfers between devices  38.9 us (17%)
  waiting for transfers between devices  24.6 us (10%)
  local copies, waits for them, and re-layouts  16.5 us (7%)
  other arithmetic  10.8 us (5%)
    pallas_call x1, Pallas kernels, shards(): pl.pallas_call(functools.partial(sum_kernel, row_count, quad_count), in_s...  72.2 us
    pallas_call x4, Pallas kernels, sweep(): pl.pallas_call(functools.partial(sweep_kernel, h, last), grid_spec=pltpu....  48.1 us
    ppermute x2, waiting for transfers between devices, shards(): pair = lax.ppermute(own, 'quad', swaps)  24.6 us
    ppermute x4, starting transfers between devices, shards(): before = lax.ppermute(iterate, 'row', up)  24 us
    pallas_call x2, Pallas kernels, mixed(): pl.pallas_call(mix_kernel, grid=(rows // tall,), in_specs=[flat_spec, fla...  8.39 us
    pallas_call x1, Pallas kernels, shards(): pl.pallas_call(functools.partial(final_kernel, CHUNKS, pairs - 1, per_dev...  8.18 us
    ppermute x2, starting transfers between devices, shards(): lax.ppermute(mixed(own, pair, send_mix[d - 1]), 'quad', route)  7.45 us
    slice x5, local copies, waits for them, and re-layouts, shards(): rhs_parts[:, p, c]  6.53 us
  transfers between devices with their start and end apart: 12, of which 2 were waited for; matrix products, arithmetic and copies ran while one was open for 6% of the time, Pallas kernels for 56%

profile of v2, /device:TPU:0, one launch (start us, length us, event | category | flops | bytes accessed | tf_op | source)
XLA Modules:
  0.0 234.2 jit_solution(10538589734051457077)
XLA Ops:
  0.6 1.5 copy.17
  2.1 0.9 fusion.11
  3.0 0.5 copy.19
  3.5 2.4 %copy.18 = bf16[4096,1,1,32]{3,0,2,1:T(8,128)(2,1)} copy(bf16[4096,1,1,32]{0,3,2,1:T(8,128)(2,1)} %get-tuple-element.17) | data formatting | bytes 524288 | tf_op jit(solution)/shard_map/slice | solution.py:333
  5.9 2.7 %pad_maximum_fusion.rhs_ref = bf16[64,64,128]{2,1,0:T(8,128)(2,1)S(1)} fusion(bf16[64,64,32]{2,1,0:T(8,128)(2,1)S(1)} %bitcast.51, bf16[64,64,32]{2,1,0:T(8,128)(2,1)} %bitcast.52), kind=kLoop, calls=%fused_computation | loop fusion | flops 4194304 | bytes 1572864 | tf_op jit(solution)/shard_map/concatenate | solution.py:333
  8.7 2.7 %initial.2.own_ref = bf16[64,64,128]{2,1,0:T(8,128)(2,1)} custom-call(bf16[2,64,64,128]{3,2,1,0:T(8,128)(2,1)S(1)} %copy-done, bf16[64,64,128]{2,1,0:T(8,128)(2,1)S(1)} %pad_maximum_fusion.rhs_ref), custom_call_target="tpu_custom_call" | custom-call | flops 268435456 | bytes 4194304 | tf_op jit(solution)/shard_map/initial/pallas_call | solution.py:261
  11.3 1.3 collective-permute-start.1
  12.6 4.0 %collective-permute-start = (bf16[64,64,128]{2,1,0:T(8,128)(2,1)}, bf16[64,64,128]{2,1,0:T(8,128)(2,1)}, u32[]{:S(2)}, u32[]{:S(2)}) collective-permute-start(bf16[64,64,128]{2,1,0:T(8,128)(2,1)} %initial.2.own_ref), channel_id=1, source_target_pairs={{0,1},{1,2},{2,3},{3,4},{4,5},{5,6},{6,7},{8,9},{9,10},{10,11},{11... | collective-permute-start | bytes 3145736 | tf_op jit(solution)/shard_map/ppermute | solution.py:342
  16.6 1.4 copy.20
  18.0 1.4 copy.21
  19.4 2.9 %pad_maximum_fusion.1.rhs_ref = bf16[64,64,128]{2,1,0:T(8,128)(2,1)S(1)} fusion(bf16[64,64,32]{2,1,0:T(8,128)(2,1)} %bitcast.53, bf16[64,64,32]{2,1,0:T(8,128)(2,1)S(1)} %bitcast.50), kind=kLoop, calls=%fused_computation.1 | loop fusion | flops 4194304 | bytes 1572864 | tf_op jit(solution)/shard_map/concatenate | solution.py:333
  22.3 2.7 %initial.3.own_ref = bf16[64,64,128]{2,1,0:T(8,128)(2,1)} custom-call(bf16[2,64,64,128]{3,2,1,0:T(8,128)(2,1)S(1)} %copy-done, bf16[64,64,128]{2,1,0:T(8,128)(2,1)S(1)} %pad_maximum_fusion.1.rhs_ref), custom_call_target="tpu_custom_call" | custom-call | flops 268435456 | bytes 4194304 | tf_op jit(solution)/shard_map/initial/pallas_call | solution.py:261
  25.0 1.3 collective-permute-start.5
  26.3 4.2 %collective-permute-start.4 = (bf16[64,64,128]{2,1,0:T(8,128)(2,1)}, bf16[64,64,128]{2,1,0:T(8,128)(2,1)S(1)}, u32[]{:S(2)}, u32[]{:S(2)}) collective-permute-start(bf16[64,64,128]{2,1,0:T(8,128)(2,1)} %initial.3.own_ref), channel_id=1, source_target_pairs={{0,1},{1,2},{2,3},{3,4},{4,5},{5,6},{6,7},{8,9},{9,10},{10,11},{11... | collective-permute-start | bytes 3145736 | tf_op jit(solution)/shard_map/ppermute | solution.py:342
  30.6 0.1 add_multiply_fusion
  30.6 0.1 multiply_cosine_fusion.1
  30.9 0.1 broadcast_in_dim.11
  30.9 0.1 cos.38
  31.1 0.1 sin.42
  31.2 0.1 cos.41
  31.3 0.1 sin.45
  31.4 0.1 copy.16
  31.4 0.1 pad.26.clone
  31.5 0.1 add_multiply_fusion.2
  31.6 0.1 add_multiply_fusion.1
  31.7 0.1 convert_add_fusion
  31.7 0.1 maximum_maximum_fusion.coef_ref
  31.8 0.1 subtract_select_fusion.index_ref
  31.9 1.2 copy-done.3
  33.2 12.2 %sweep.4.own_ref = bf16[64,64,128]{2,1,0:T(8,128)(2,1)} custom-call(s32[64,24]{1,0:T(8,128)S(1)} %subtract_select_fusion.index_ref, bf16[64,64,1536]{2,1,0:T(8,128)(2,1)} %ham_ref.7, bf16[2,64,64,128]{3,2,1,0:T(8,128)(2,1)} %pre_ref.11, bf16[64,64,128]{2,1,0:T(8,128)(2,1)S(1)} %copy-done.3, bf16[64,64,128]{2,1,0:T(8,128)(2,1)S(1)} %bitcast.40, ...), custom_call_target="tpu_custom_call" | custom-call | flops 1610612736 | bytes 17825792 | tf_op jit(solution)/shard_map/sweep/pallas_call | solution.py:280
  45.4 1.3 collective-permute-start.3
  46.7 8.1 %collective-permute-start.2 = (bf16[64,64,128]{2,1,0:T(8,128)(2,1)}, bf16[64,64,128]{2,1,0:T(8,128)(2,1)}, u32[]{:S(2)}, u32[]{:S(2)}) collective-permute-start(bf16[64,64,128]{2,1,0:T(8,128)(2,1)} %sweep.4.own_ref), channel_id=1, source_target_pairs={{0,1},{1,2},{2,3},{3,4},{4,5},{5,6},{6,7},{8,9},{9,10},{10,11},{11... | collective-permute-start | bytes 3145736 | tf_op jit(solution)/shard_map/ppermute | solution.py:342
  54.9 12.0 %sweep.6.own_ref = bf16[64,64,128]{2,1,0:T(8,128)(2,1)} custom-call(s32[64,24]{1,0:T(8,128)S(1)} %subtract_select_fusion.index_ref, bf16[64,64,1536]{2,1,0:T(8,128)(2,1)} %ham_ref.7, bf16[2,64,64,128]{3,2,1,0:T(8,128)(2,1)} %pre_ref.11, bf16[64,64,128]{2,1,0:T(8,128)(2,1)S(1)} %copy-done.6, bf16[64,64,128]{2,1,0:T(8,128)(2,1)S(1)} %bitcast.41, ...), custom_call_target="tpu_custom_call" | custom-call | flops 1610612736 | bytes 17825792 | tf_op jit(solution)/shard_map/sweep/pallas_call | solution.py:280
  66.9 1.4 collective-permute-start.7
  68.3 7.7 %collective-permute-start.6 = (bf16[64,64,128]{2,1,0:T(8,128)(2,1)}, bf16[64,64,128]{2,1,0:T(8,128)(2,1)}, u32[]{:S(2)}, u32[]{:S(2)}) collective-permute-start(bf16[64,64,128]{2,1,0:T(8,128)(2,1)} %sweep.6.own_ref), channel_id=1, source_target_pairs={{0,1},{1,2},{2,3},{3,4},{4,5},{5,6},{6,7},{8,9},{9,10},{10,11},{11... | collective-permute-start | bytes 3145736 | tf_op jit(solution)/shard_map/ppermute | solution.py:342
  76.0 0.2 fusion.10
  76.2 0.1 maximum_bitcast_fusion.3
  76.3 1.0 multiply_bitcast_fusion.1
  77.3 1.5 reshape.357
  78.8 12.0 %sweep.5 = (bf16[64,64,128]{2,1,0:T(8,128)(2,1)S(1)}, f32[128,128]{1,0:T(8,128)S(1)}) custom-call(s32[64,24]{1,0:T(8,128)S(1)} %subtract_select_fusion.index_ref, bf16[64,64,1536]{2,1,0:T(8,128)(2,1)} %ham_ref.7, bf16[2,64,64,128]{3,2,1,0:T(8,128)(2,1)} %pre_ref.11, bf16[64,64,128]{2,1,0:T(8,128)(2,1)S(1)} %copy-done.4, bf16[64,64,128]{2,1,0:T(8,128)(2,1)S(1)} %bitcast.42, ...), custom_call_target="tpu_custom_call" | custom-call | flops 1610612736 | bytes 17825792 | tf_op jit(solution)/shard_map/sweep/pallas_call | solution.py:280
  90.8 1.6 collective-permute-start.8
  92.5 12.0 %sweep.7 = (bf16[64,64,128]{2,1,0:T(8,128)(2,1)S(1)}, f32[128,128]{1,0:T(8,128)S(1)}) custom-call(s32[64,24]{1,0:T(8,128)S(1)} %subtract_select_fusion.index_ref, bf16[64,64,1536]{2,1,0:T(8,128)(2,1)} %ham_ref.7, bf16[2,64,64,128]{3,2,1,0:T(8,128)(2,1)} %pre_ref.11, bf16[64,64,128]{2,1,0:T(8,128)(2,1)S(1)} %copy-done.6, bf16[64,64,128]{2,1,0:T(8,128)(2,1)S(1)} %bitcast.43, ...), custom_call_target="tpu_custom_call" | custom-call | flops 1610612736 | bytes 17825792 | tf_op jit(solution)/shard_map/sweep/pallas_call | solution.py:280
  104.5 0.5 collective-permute-start.9
  105.1 0.1 compare_convert_fusion
  105.1 10.1 %collective-permute-done.8.pair_ref.refs_2_ = bf16[4096,128]{1,0:T(8,128)(2,1)S(1)} collective-permute-done((bf16[4096,128]{1,0:T(8,128)(2,1)S(1)}, bf16[4096,128]{1,0:T(8,128)(2,1)S(1)}, u32[]{:S(2)}, u32[]{:S(2)}) %collective-permute-start.8) | collective-permute-done | bytes 1048608 | tf_op jit(solution)/shard_map/ppermute | solution.py:349
  115.2 4.2 %mixed.2 = bf16[4096,128]{1,0:T(8,128)(2,1)} custom-call(bf16[4096,128]{1,0:T(8,128)(2,1)S(1)} %bitcast.45, bf16[4096,128]{1,0:T(8,128)(2,1)S(1)} %collective-permute-done.8.pair_ref.refs_2_, bf16[2,256,128]{2,1,0:T(8,128)(2,1)S(1)} %maximum_bitcast_fusion.1.mix_ref), custom_call_target="tpu_custom_call" | custom-call | flops 536870912 | bytes 3145728 | tf_op jit(solution)/shard_map/mixed/pallas_call | solution.py:319
  119.4 3.6 %collective-permute-start.10 = (bf16[4096,128]{1,0:T(8,128)(2,1)}, bf16[4096,128]{1,0:T(8,128)(2,1)}, u32[]{:S(2)}, u32[]{:S(2)}) collective-permute-start(bf16[4096,128]{1,0:T(8,128)(2,1)} %mixed.2), channel_id=1, source_target_pairs={{0,24},{8,16},{16,8},{24,0},{1,25},{9,17},{17,9},{25,1},{2,26},{10... | collective-permute-start | bytes 3145736 | tf_op jit(solution)/shard_map/ppermute | solution.py:357
  123.0 14.5 %collective-permute-done.9.pair_ref.refs_3_ = bf16[4096,128]{1,0:T(8,128)(2,1)S(1)} collective-permute-done((bf16[4096,128]{1,0:T(8,128)(2,1)S(1)}, bf16[4096,128]{1,0:T(8,128)(2,1)S(1)}, u32[]{:S(2)}, u32[]{:S(2)}) %collective-permute-start.9) | collective-permute-done | bytes 1048608 | tf_op jit(solution)/shard_map/ppermute | solution.py:349
  137.5 4.2 %mixed.3 = bf16[4096,128]{1,0:T(8,128)(2,1)} custom-call(bf16[4096,128]{1,0:T(8,128)(2,1)S(1)} %bitcast.48, bf16[4096,128]{1,0:T(8,128)(2,1)S(1)} %collective-permute-done.9.pair_ref.refs_3_, bf16[2,256,128]{2,1,0:T(8,128)(2,1)S(1)} %maximum_bitcast_fusion.1.mix_ref), custom_call_target="tpu_custom_call" | custom-call | flops 536870912 | bytes 3145728 | tf_op jit(solution)/shard_map/mixed/pallas_call | solution.py:319
  141.7 3.8 %collective-permute-start.11 = (bf16[4096,128]{1,0:T(8,128)(2,1)}, bf16[4096,128]{1,0:T(8,128)(2,1)}, u32[]{:S(2)}, u32[]{:S(2)}) collective-permute-start(bf16[4096,128]{1,0:T(8,128)(2,1)} %mixed.3), channel_id=1, source_target_pairs={{0,24},{8,16},{16,8},{24,0},{1,25},{9,17},{17,9},{25,1},{2,26},{10... | collective-permute-start | bytes 3145736 | tf_op jit(solution)/shard_map/ppermute | solution.py:357
  145.6 0.2 fusion
  145.8 0.2 convert_element_type.133.refs_7_
  146.0 0.5 multiply_bitcast_fusion
  146.5 1.7 reshape.358
  148.2 1.4 subtract_convert_fusion
  149.6 0.9 maximum_bitcast_fusion.refs_6_
  150.5 0.1 copy.24
  150.6 0.1 copy.25
  150.8 0.1 copy.27.terms_ref
  150.9 72.2 %sum_blocks.1 = f32[2,128,128]{2,1,0:T(8,128)S(1)} custom-call(f32[2,16]{1,0:T(2,128)S(1)} %maximum_multiply_fusion.coef_ref, f32[128,256]{1,0:T(8,128)S(1)} %copy.27.terms_ref), custom_call_target="tpu_custom_call" | custom-call | bytes 41943040 | tf_op jit(solution)/shard_map/sum_blocks/pallas_call | solution.py:367
  223.1 1.2 copy-done.14
  224.4 1.0 copy-done.15
  225.4 8.2 %final.1 = f32[2,4096,128]{2,1,0:T(8,128)} custom-call(bf16[4096,128]{1,0:T(8,128)(2,1)S(1)} %bitcast.46, bf16[4096,128]{1,0:T(8,128)(2,1)S(1)} %bitcast.49, bf16[4096,128]{1,0:T(8,128)(2,1)S(1)} %copy-done.10, bf16[4096,128]{1,0:T(8,128)(2,1)S(1)} %copy-done.14, bf16[4096,128]{1,0:T(8,128)(2,1)} %collective-permute-done.10.refs_4_, ...), custom_call_target="tpu_custom_call" | custom-call | tf_op jit(solution)/shard_map/final/pallas_call | solution.py:388
  233.6 0.7 copy.33
  (61 shorter events, 0.4 us)
Async XLA Ops:
  3.5 5.2 %copy-start = (bf16[2,64,64,128]{3,2,1,0:T(8,128)(2,1)S(1)}, bf16[2,64,64,128]{3,2,1,0:T(8,128)(2,1)}, u32[]{:S(2)}) copy-start(bf16[2,64,64,128]{3,2,1,0:T(8,128)(2,1)} %pre_ref.11) | copy-start | bytes 6291460
  8.7 2.7 %copy-start.2 = (bf16[64,64,128]{2,1,0:T(8,128)(2,1)}, bf16[64,64,128]{2,1,0:T(8,128)(2,1)S(1)}, u32[]{:S(2)}) copy-start(bf16[64,64,128]{2,1,0:T(8,128)(2,1)S(1)} %pad_maximum_fusion.rhs_ref) | copy-start | bytes 3145732
  11.3 20.6 %collective-permute-start.1 = (bf16[64,64,128]{2,1,0:T(8,128)(2,1)}, bf16[64,64,128]{2,1,0:T(8,128)(2,1)}, u32[]{:S(2)}, u32[]{:S(2)}) collective-permute-start(bf16[64,64,128]{2,1,0:T(8,128)(2,1)} %initial.2.own_ref), channel_id=1, source_target_pairs={{1,0},{2,1},{3,2},{4,3},{5,4},{6,5},{7,6},{9,8},{10,9},{11,10},{12... | collective-permute-start | bytes 3145736 | tf_op jit(solution)/shard_map/ppermute | solution.py:343
  12.6 19.3 %collective-permute-start = (bf16[64,64,128]{2,1,0:T(8,128)(2,1)}, bf16[64,64,128]{2,1,0:T(8,128)(2,1)}, u32[]{:S(2)}, u32[]{:S(2)}) collective-permute-start(bf16[64,64,128]{2,1,0:T(8,128)(2,1)} %initial.2.own_ref), channel_id=1, source_target_pairs={{0,1},{1,2},{2,3},{3,4},{4,5},{5,6},{6,7},{8,9},{9,10},{10,11},{11... | collective-permute-start | bytes 3145736 | tf_op jit(solution)/shard_map/ppermute | solution.py:342
  22.3 2.7 %copy-start.5 = (bf16[64,64,128]{2,1,0:T(8,128)(2,1)}, bf16[64,64,128]{2,1,0:T(8,128)(2,1)S(1)}, u32[]{:S(2)}) copy-start(bf16[64,64,128]{2,1,0:T(8,128)(2,1)S(1)} %pad_maximum_fusion.1.rhs_ref) | copy-start | bytes 3145732
  22.3 9.1 %copy-start.16 = (s32[64,24]{0,1:T(8,128)S(1)}, s32[64,24]{0,1:T(8,128)}, u32[]{:S(2)}) copy-start(s32[64,24]{0,1:T(8,128)} %param.6) | copy-start | bytes 18436
  22.3 9.5 %copy-start.17 = (s32[64]{0:T(128)S(1)}, s32[64]{0:T(128)}, u32[]{:S(2)}) copy-start(s32[64]{0:T(128)} %param.7) | copy-start | bytes 772
  22.3 9.6 %copy-start.1 = (bf16[4096,128]{1,0:T(8,128)(2,1)S(1)}, bf16[4096,128]{1,0:T(8,128)(2,1)}, u32[]{:S(2)}) copy-start(bf16[4096,128]{1,0:T(8,128)(2,1)} %param.9) | copy-start | bytes 3145732
  25.0 29.9 %collective-permute-start.5 = (bf16[64,64,128]{2,1,0:T(8,128)(2,1)}, bf16[64,64,128]{2,1,0:T(8,128)(2,1)}, u32[]{:S(2)}, u32[]{:S(2)}) collective-permute-start(bf16[64,64,128]{2,1,0:T(8,128)(2,1)} %initial.3.own_ref), channel_id=1, source_target_pairs={{1,0},{2,1},{3,2},{4,3},{5,4},{6,5},{7,6},{9,8},{10,9},{11,10},{12... | collective-permute-start | bytes 3145736 | tf_op jit(solution)/shard_map/ppermute | solution.py:343
  26.3 28.6 %collective-permute-start.4 = (bf16[64,64,128]{2,1,0:T(8,128)(2,1)}, bf16[64,64,128]{2,1,0:T(8,128)(2,1)S(1)}, u32[]{:S(2)}, u32[]{:S(2)}) collective-permute-start(bf16[64,64,128]{2,1,0:T(8,128)(2,1)} %initial.3.own_ref), channel_id=1, source_target_pairs={{0,1},{1,2},{2,3},{3,4},{4,5},{5,6},{6,7},{8,9},{9,10},{10,11},{11... | collective-permute-start | bytes 3145736 | tf_op jit(solution)/shard_map/ppermute | solution.py:342
  31.9 1.2 copy-start.3
  33.2 21.7 %copy-start.6 = (bf16[64,64,128]{2,1,0:T(8,128)(2,1)S(1)}, bf16[64,64,128]{2,1,0:T(8,128)(2,1)}, u32[]{:S(2)}) copy-start(bf16[64,64,128]{2,1,0:T(8,128)(2,1)} %copy-done.5) | copy-start | bytes 3145732
  45.4 33.4 %collective-permute-start.3 = (bf16[64,64,128]{2,1,0:T(8,128)(2,1)}, bf16[64,64,128]{2,1,0:T(8,128)(2,1)}, u32[]{:S(2)}, u32[]{:S(2)}) collective-permute-start(bf16[64,64,128]{2,1,0:T(8,128)(2,1)} %sweep.4.own_ref), channel_id=1, source_target_pairs={{1,0},{2,1},{3,2},{4,3},{5,4},{6,5},{7,6},{9,8},{10,9},{11,10},{12... | collective-permute-start | bytes 3145736 | tf_op jit(solution)/shard_map/ppermute | solution.py:343
  46.7 32.1 %collective-permute-start.2 = (bf16[64,64,128]{2,1,0:T(8,128)(2,1)}, bf16[64,64,128]{2,1,0:T(8,128)(2,1)}, u32[]{:S(2)}, u32[]{:S(2)}) collective-permute-start(bf16[64,64,128]{2,1,0:T(8,128)(2,1)} %sweep.4.own_ref), channel_id=1, source_target_pairs={{0,1},{1,2},{2,3},{3,4},{4,5},{5,6},{6,7},{8,9},{9,10},{10,11},{11... | collective-permute-start | bytes 3145736 | tf_op jit(solution)/shard_map/ppermute | solution.py:342
  66.8 12.0 %copy-start.4 = (bf16[64,64,128]{2,1,0:T(8,128)(2,1)S(1)}, bf16[64,64,128]{2,1,0:T(8,128)(2,1)}, u32[]{:S(2)}) copy-start(bf16[64,64,128]{2,1,0:T(8,128)(2,1)} %copy-done.2) | copy-start | bytes 3145732
  66.9 25.6 %collective-permute-start.7 = (bf16[64,64,128]{2,1,0:T(8,128)(2,1)}, bf16[64,64,128]{2,1,0:T(8,128)(2,1)}, u32[]{:S(2)}, u32[]{:S(2)}) collective-permute-start(bf16[64,64,128]{2,1,0:T(8,128)(2,1)} %sweep.6.own_ref), channel_id=1, source_target_pairs={{1,0},{2,1},{3,2},{4,3},{5,4},{6,5},{7,6},{9,8},{10,9},{11,10},{12... | collective-permute-start | bytes 3145736 | tf_op jit(solution)/shard_map/ppermute | solution.py:343
  68.3 24.2 %collective-permute-start.6 = (bf16[64,64,128]{2,1,0:T(8,128)(2,1)}, bf16[64,64,128]{2,1,0:T(8,128)(2,1)}, u32[]{:S(2)}, u32[]{:S(2)}) collective-permute-start(bf16[64,64,128]{2,1,0:T(8,128)(2,1)} %sweep.6.own_ref), channel_id=1, source_target_pairs={{0,1},{1,2},{2,3},{3,4},{4,5},{5,6},{6,7},{8,9},{9,10},{10,11},{11... | collective-permute-start | bytes 3145736 | tf_op jit(solution)/shard_map/ppermute | solution.py:342
  90.8 24.4 %copy-start.7 = (bf16[64,64,128]{2,1,0:T(8,128)(2,1)}, bf16[64,64,128]{2,1,0:T(8,128)(2,1)S(1)}, u32[]{:S(2)}) copy-start(bf16[64,64,128]{2,1,0:T(8,128)(2,1)S(1)} %get-tuple-element.6) | copy-start | bytes 3145732
  90.8 24.4 %collective-permute-start.8 = (bf16[4096,128]{1,0:T(8,128)(2,1)S(1)}, bf16[4096,128]{1,0:T(8,128)(2,1)S(1)}, u32[]{:S(2)}, u32[]{:S(2)}) collective-permute-start(bf16[4096,128]{1,0:T(8,128)(2,1)S(1)} %bitcast.44), channel_id=1, source_target_pairs={{0,8},{8,0},{16,24},{24,16},{1,9},{9,1},{17,25},{25,17},{2,10},{10... | collective-permute-start | bytes 3145736 | tf_op jit(solution)/shard_map/ppermute | solution.py:349
  104.5 37.3 %copy-start.11 = (bf16[64,64,128]{2,1,0:T(8,128)(2,1)}, bf16[64,64,128]{2,1,0:T(8,128)(2,1)S(1)}, u32[]{:S(2)}) copy-start(bf16[64,64,128]{2,1,0:T(8,128)(2,1)S(1)} %get-tuple-element.7) | copy-start | bytes 3145732
  104.5 33.0 %collective-permute-start.9 = (bf16[4096,128]{1,0:T(8,128)(2,1)S(1)}, bf16[4096,128]{1,0:T(8,128)(2,1)S(1)}, u32[]{:S(2)}, u32[]{:S(2)}) collective-permute-start(bf16[4096,128]{1,0:T(8,128)(2,1)S(1)} %bitcast.47), channel_id=1, source_target_pairs={{0,8},{8,0},{16,24},{24,16},{1,9},{9,1},{17,25},{25,17},{2,10},{10... | collective-permute-start | bytes 3145736 | tf_op jit(solution)/shard_map/ppermute | solution.py:349
  115.2 26.5 %copy-start.9 = (bf16[4096,128]{1,0:T(8,128)(2,1)}, bf16[4096,128]{1,0:T(8,128)(2,1)S(1)}, u32[]{:S(2)}) copy-start(bf16[4096,128]{1,0:T(8,128)(2,1)S(1)} %collective-permute-done.8.pair_ref.refs_2_) | copy-start | bytes 3145732
  119.4 103.7 %collective-permute-start.10 = (bf16[4096,128]{1,0:T(8,128)(2,1)}, bf16[4096,128]{1,0:T(8,128)(2,1)}, u32[]{:S(2)}, u32[]{:S(2)}) collective-permute-start(bf16[4096,128]{1,0:T(8,128)(2,1)} %mixed.2), channel_id=1, source_target_pairs={{0,24},{8,16},{16,8},{24,0},{1,25},{9,17},{17,9},{25,1},{2,26},{10... | collective-permute-start | bytes 3145736 | tf_op jit(solution)/shard_map/ppermute | solution.py:357
  137.5 8.1 %copy-start.13 = (bf16[4096,128]{1,0:T(8,128)(2,1)}, bf16[4096,128]{1,0:T(8,128)(2,1)S(1)}, u32[]{:S(2)}) copy-start(bf16[4096,128]{1,0:T(8,128)(2,1)S(1)} %collective-permute-done.9.pair_ref.refs_3_) | copy-start | bytes 3145732
  141.7 81.4 %collective-permute-start.11 = (bf16[4096,128]{1,0:T(8,128)(2,1)}, bf16[4096,128]{1,0:T(8,128)(2,1)}, u32[]{:S(2)}, u32[]{:S(2)}) collective-permute-start(bf16[4096,128]{1,0:T(8,128)(2,1)} %mixed.3), channel_id=1, source_target_pairs={{0,24},{8,16},{16,8},{24,0},{1,25},{9,17},{17,9},{25,1},{2,26},{10... | collective-permute-start | bytes 3145736 | tf_op jit(solution)/shard_map/ppermute | solution.py:357
  148.2 74.9 %copy-start.8 = (bf16[64,64,128]{2,1,0:T(8,128)(2,1)S(1)}, bf16[64,64,128]{2,1,0:T(8,128)(2,1)}, u32[]{:S(2)}) copy-start(bf16[64,64,128]{2,1,0:T(8,128)(2,1)} %copy-done.7) | copy-start | bytes 3145732
  148.2 74.9 %copy-start.10 = (bf16[4096,128]{1,0:T(8,128)(2,1)S(1)}, bf16[4096,128]{1,0:T(8,128)(2,1)}, u32[]{:S(2)}) copy-start(bf16[4096,128]{1,0:T(8,128)(2,1)} %copy-done.9) | copy-start | bytes 3145732
  148.2 74.9 %copy-start.12 = (bf16[64,64,128]{2,1,0:T(8,128)(2,1)S(1)}, bf16[64,64,128]{2,1,0:T(8,128)(2,1)}, u32[]{:S(2)}) copy-start(bf16[64,64,128]{2,1,0:T(8,128)(2,1)} %copy-done.11) | copy-start | bytes 3145732
  223.1 1.2 copy-start.14
  224.4 1.0 copy-start.15
